TPU v7x, 32 devices: a whole 2x2x4 slice. The times are simulated.
32 devices in a mesh: dp: 4 (over z), expert: 8 (over y, x, core).
Axes of the slice: x: 2, y: 2, z: 4, core: 2. Of those that a mesh axis runs over, the one named last changes fastest.
Arguments:
- tokens: bfloat16 [8192, 2048], P(('dp', 'expert')), may hold values from -6 to 6
- expert_ids: int32 [8192, 4], P(('dp', 'expert')), may hold values from 0 to 7, as said below
- gates: float32 [8192, 4], P(('dp', 'expert')), may hold values from 0.1 to 1
- w_gate: bfloat16 [8, 2048, 384], P('expert'), may hold values from -0.125 to 0.125
- w_up: bfloat16 [8, 2048, 384], P('expert'), may hold values from -0.125 to 0.125
- w_down: bfloat16 [8, 2048, 384], P('expert'), may hold values from -0.3125 to 0.3125
- cotangent: bfloat16 [8192, 2048], P(('dp', 'expert')), may hold values from -6 to 6
Outputs:
- mixed: bfloat16 [8192, 2048], P(('dp', 'expert'))
- tokens_grad: bfloat16 [8192, 2048], P(('dp', 'expert'))
- gates_grad: float32 [8192, 4], P(('dp', 'expert'))
- gate_grad: float32 [8, 2048, 384], P('expert', 'dp')
- up_grad: float32 [8, 2048, 384], P('expert', 'dp')
- down_grad: float32 [8, 2048, 384], P('expert', 'dp')
Inputs may be any that keep to these rules, and one draw needn't show every extreme that they name: `expert_ids`: each row holds 4 different experts. One expert, the same in every draw position, is named by every token. Among the 256 tokens of one device every other expert is named at most 110 times, and one of them is named exactly 110 times on every device.
All inputs are finite; a program needn't handle non-finite values.
Results may differ from a plain program's by a relative error of at most 0.014.
Values may be sent and summed in bfloat16 or wider, within the bound.
No kernel may reach another device: no remote copies, remote signals or barrier semaphores. Data moves between devices by JAX's collectives and lax.ppermute only.
A program may use at most 128 MiB of HBM per device.

v0:
```python
import jax
import jax.numpy as jnp
from jax import lax
from jax.sharding import PartitionSpec as P

D = 2048
FF = 384
TOPK = 4


def broadcast(value, axis, source):
    kept = jnp.where(lax.axis_index(axis) == source, value, 0).astype(value.dtype)
    return lax.psum(kept, axis)


def expert_forward(rows, weight_gate, weight_up, weight_down):
    gate_act = jnp.dot(rows, weight_gate, preferred_element_type=jnp.float32)
    up_act = jnp.dot(rows, weight_up, preferred_element_type=jnp.float32)
    hidden = (jax.nn.silu(gate_act) * up_act).astype(jnp.bfloat16)
    output = lax.dot_general(
        hidden, weight_down, (((1,), (1,)), ((), ())), preferred_element_type=jnp.float32
    ).astype(jnp.bfloat16)
    return (gate_act, up_act, hidden, output)


def expert_backward(rows, upstream, weight_gate, weight_up, weight_down, gate_act, up_act, hidden):
    hidden_grad = jnp.dot(upstream, weight_down, preferred_element_type=jnp.float32)
    sigma = jax.nn.sigmoid(gate_act)
    gate_pre = (hidden_grad * up_act * sigma * (1.0 + gate_act * (1.0 - sigma))).astype(
        jnp.bfloat16
    )
    up_pre = (hidden_grad * gate_act * sigma).astype(jnp.bfloat16)
    contract = (((1,), (1,)), ((), ()))
    input_part = (
        lax.dot_general(gate_pre, weight_gate, contract, preferred_element_type=jnp.float32)
        + lax.dot_general(up_pre, weight_up, contract, preferred_element_type=jnp.float32)
    ).astype(jnp.bfloat16)
    over_rows = (((0,), (0,)), ((), ()))
    grad_gate = lax.dot_general(rows, gate_pre, over_rows, preferred_element_type=jnp.float32)
    grad_upper = lax.dot_general(rows, up_pre, over_rows, preferred_element_type=jnp.float32)
    grad_down = lax.dot_general(upstream, hidden, over_rows, preferred_element_type=jnp.float32)
    return (input_part, grad_gate, grad_upper, grad_down)


def per_device(tokens, expert_ids, gates, w_gate, w_up, w_down, cotangent):
    experts = lax.axis_size("expert")
    tok_rows = tokens.shape[0]
    capacity = (tok_rows * (TOPK - 1) + experts - 2) // (experts - 1)
    over_rows = (((0,), (0,)), ((), ()))
    highest = lax.Precision.HIGHEST
    expert_range = jnp.arange(experts, dtype=jnp.int32)
    matches = (expert_ids[:, :, None] == expert_range).astype(jnp.int32)
    counts = jnp.sum(matches, axis=(0, 1))
    hot_expert = jnp.argmax(counts)
    is_hot = expert_ids == hot_expert
    flat_matches = matches.reshape(tok_rows * TOPK, experts)
    before = jnp.cumsum(flat_matches, axis=0) - flat_matches
    position = jnp.sum(before * flat_matches, axis=1)
    target = jnp.where(is_hot.reshape(-1), -1, expert_ids.reshape(-1) * capacity + position)
    slot_ids = jnp.arange(experts * capacity, dtype=jnp.int32)
    dispatch_f = (slot_ids[:, None] == target[None, :]).astype(jnp.float32)
    per_token_f = jnp.sum(dispatch_f.reshape(experts * capacity, tok_rows, TOPK), axis=2)
    per_token = per_token_f.astype(jnp.bfloat16)
    slot_gate = jnp.dot(
        dispatch_f, gates.reshape(-1), precision=highest, preferred_element_type=jnp.float32
    )
    own_weights = (w_gate[0], w_up[0], w_down[0])
    shadow = (
        broadcast(own_weights[0], "expert", hot_expert),
        broadcast(own_weights[1], "expert", hot_expert),
        broadcast(own_weights[2], "expert", hot_expert),
    )
    outgoing = jnp.dot(per_token, tokens, preferred_element_type=jnp.float32).astype(jnp.bfloat16)
    outgoing = outgoing.reshape(experts, capacity, D)
    rows = lax.all_to_all(outgoing, "expert", split_axis=0, concat_axis=0, tiled=True)
    leading = rows.shape[:2]
    gate_act, up_act, hidden, output = expert_forward(rows.reshape(-1, D), *own_weights)
    received, expert_out, gate_act, up_act, hidden = (
        rows,
        output.reshape(leading + (D,)),
        gate_act.reshape(leading + (FF,)),
        up_act.reshape(leading + (FF,)),
        hidden.reshape(leading + (FF,)),
    )
    returned = lax.all_to_all(expert_out, "expert", split_axis=0, concat_axis=0, tiled=True)
    hot_gate, hot_up, hot_hidden, hot_out = expert_forward(tokens, *shadow)
    returned_f = returned.reshape(-1, D).astype(jnp.float32)
    weighted = slot_gate[:, None] * returned_f
    mixed_cold = lax.dot_general(
        per_token_f, weighted, over_rows, precision=highest, preferred_element_type=jnp.float32
    )
    hot_weight = jnp.sum(jnp.where(is_hot, gates, 0.0), axis=1)
    hot_out_f = hot_out.astype(jnp.float32)
    mixed = (mixed_cold + hot_weight[:, None] * hot_out_f).astype(jnp.bfloat16)
    upstream = cotangent.astype(jnp.float32)
    copied = jnp.dot(per_token, cotangent, preferred_element_type=jnp.float32)
    slot_dot = jnp.sum(returned_f * copied, axis=1)
    cold_gates = jnp.dot(
        slot_dot, dispatch_f, precision=highest, preferred_element_type=jnp.float32
    ).reshape(tok_rows, TOPK)
    hot_dot = jnp.sum(upstream * hot_out_f, axis=1)
    gates_grad = cold_gates + jnp.where(is_hot, hot_dot[:, None], 0.0)
    outgoing_grad = (slot_gate[:, None] * copied).astype(jnp.bfloat16)
    incoming_grad = lax.all_to_all(
        outgoing_grad.reshape(experts, capacity, D),
        "expert",
        split_axis=0,
        concat_axis=0,
        tiled=True,
    )
    input_rows, own_gate, own_upper, own_down = expert_backward(
        received.reshape(-1, D),
        incoming_grad.reshape(-1, D),
        *own_weights,
        gate_act.reshape(-1, FF),
        up_act.reshape(-1, FF),
        hidden.reshape(-1, FF)
    )
    back_rows = lax.all_to_all(
        input_rows.reshape(experts, capacity, D), "expert", split_axis=0, concat_axis=0, tiled=True
    )
    cold_input = lax.dot_general(
        per_token, back_rows.reshape(-1, D), over_rows, preferred_element_type=jnp.float32
    )
    hot_upstream = (hot_weight[:, None] * upstream).astype(jnp.bfloat16)
    hot_input, hot_gate_grad, hot_upper_grad, hot_down_grad = expert_backward(
        tokens, hot_upstream, *shadow, hot_gate, hot_up, hot_hidden
    )
    tokens_grad = (cold_input + hot_input.astype(jnp.float32)).astype(jnp.bfloat16)
    own_part = jnp.stack([own_gate, own_upper, own_down])
    hot_part = jnp.stack([hot_gate_grad, hot_upper_grad, hot_down_grad])
    is_owner = lax.axis_index("expert") == hot_expert
    own_sum = lax.psum_scatter(own_part, "dp", scatter_dimension=1, tiled=True)
    pieces = lax.psum_scatter(hot_part, ("dp", "expert"), scatter_dimension=1, tiled=True)
    shadow_sum = lax.all_gather(pieces.astype(jnp.bfloat16), "expert", axis=1, tiled=True).astype(
        pieces.dtype
    )
    grads = own_sum + jnp.where(is_owner, shadow_sum, 0.0)
    return (mixed, tokens_grad, gates_grad, grads[0][None], grads[1][None], grads[2][None])


def solution(mesh):
    return jax.shard_map(
        per_device,
        mesh=mesh,
        in_specs=(
            P(("dp", "expert"), None),
            P(("dp", "expert"), None),
            P(("dp", "expert"), None),
            P("expert", None, None),
            P("expert", None, None),
            P("expert", None, None),
            P(("dp", "expert"), None),
        ),
        out_specs=(
            P(("dp", "expert"), None),
            P(("dp", "expert"), None),
            P(("dp", "expert"), None),
            P("expert", "dp", None),
            P("expert", "dp", None),
            P("expert", "dp", None),
        ),
        check_vma=False,
    )
```

profile of v0, /device:TPU:0, one launch (start us, length us, event | category | flops | bytes accessed | tf_op | source)
XLA Modules:
  0.0 509.0 jit_solution(7187236622559245649)
XLA Ops:
  8.1 1.0 convert_reduce_fusion.1
  10.4 2.9 bitcast_select_fusion
  13.3 2.0 bitcast_select_fusion.1
  16.3 2.3 reduce-window.6
  20.0 85.3 %all-reduce.3.cloned.1.call-done = (bf16[2048,384]{1,0:T(8,128)(2,1)}, bf16[2048,384]{1,0:T(8,128)(2,1)}, bf16[2048,384]{1,0:T(8,128)(2,1)}) async-done(((bf16[2048,384]{1,0:T(8,128)(2,1)}, bf16[2048,384]{1,0:T(8,128)(2,1)}, bf16[2048,384]{1,0:T(8,128)(2,1)}), (bf16[2048,384]{1,0:T(8,128)(2,1)}, bf16[2048,384]{1,0:T(8,128)(2,1)}, bf16[2048,384]{1,0:T(8,128)(2,1)})) %all-reduce.3.cloned.1.call-update) | async-done | bytes 4718608 | tf_op jit(solution)/shard_map/psum | solution.py:13
  105.3 2.1 convolution_bitcast_fusion.7
  109.2 1.0 multiply_convert_fusion.4
  110.2 0.8 convolution_bitcast_fusion
  111.1 0.8 convolution_bitcast_fusion.1
  111.8 0.8 convolution_bitcast_fusion.2
  112.6 4.1 pad_maximum_fusion.1
  117.3 2.9 convolution_convert_fusion
  120.2 3.8 reshape.98
  124.1 48.5 %all_to_all.20 = bf16[8,110,2048]{2,1,0:T(8,128)(2,1)} all-to-all(bf16[8,110,2048]{2,1,0:T(8,128)(2,1)} %reshape.98), channel_id=1, replica_groups=mesh['dp'=4,'expert'=8] {'expert'}, dimensions={0} | all-to-all | bytes 7208960 | tf_op jit(solution)/shard_map/all_to_all | solution.py:75
  172.6 3.8 reshape.99
  176.4 4.7 fusion.25
  181.1 3.2 multiply_convert_fusion.3
  184.3 3.9 convolution_convert_fusion.1
  188.2 3.8 reshape.100
  192.0 4.5 all-to-all-start.1
  197.2 1.7 fusion.27
  198.9 48.2 %all-to-all-done.1 = bf16[8,110,2048]{2,1,0:T(8,128)(2,1)} async-done(((bf16[8,110,2048]{2,1,0:T(8,128)(2,1)}), bf16[8,110,2048]{2,1,0:T(8,128)(2,1)}, u32[]{:S(2)}, u32[]{:S(2)}) %all-to-all-start.1) | async-done | bytes 3604512 | tf_op jit(solution)/shard_map/all_to_all | solution.py:85
  247.1 4.9 reshape.105
  252.0 6.1 %multiply_reduce_fusion = (f32[880]{0:T(1024)S(1)}, bf16[880,2048]{1,0:T(8,128)(2,1)}) fusion(f32[880,2048]{1,0:T(8,128)} %reshape.105, f32[880]{0:T(1024)S(1)} %fusion.27, bf16[256,2048]{1,0:T(8,128)(2,1)S(1)} %copy-done.2, f32[880,256]{1,0:T(8,128)S(1)} %convert_reduce_fusion), kind=kOutput, calls=%fused_computation.2 | convolution fusion | flops 930180224 | bytes 12770176 | tf_op jit(solution)/shard_map/dot_general | solution.py:96
  258.1 3.9 reshape.101
  262.0 49.6 %all_to_all.21 = bf16[8,110,2048]{2,1,0:T(8,128)(2,1)} all-to-all(bf16[8,110,2048]{2,1,0:T(8,128)(2,1)} %reshape.101), channel_id=1, replica_groups=mesh['dp'=4,'expert'=8] {'expert'}, dimensions={0} | all-to-all | bytes 7208960 | tf_op jit(solution)/shard_map/all_to_all | solution.py:104
  311.6 3.9 reshape.102
  315.4 5.9 %convolution_bitcast_fusion.3 = f32[1,2048,384]{2,1,0:T(8,128)} fusion(bf16[880,2048]{1,0:T(8,128)(2,1)} %reshape.102, bf16[880,384]{1,0:T(8,128)(2,1)S(1)} %get-tuple-element.35), kind=kOutput, calls=%fused_computation.20 | convolution fusion | flops 1384120320 | bytes 7426048 | tf_op jit(solution)/shard_map/dot_general | solution.py:41
  321.3 1.6 convert_element_type.112
  323.3 5.8 %multiply_convert_fusion.1 = (bf16[880,384]{1,0:T(8,128)(2,1)S(1)}, bf16[880,384]{1,0:T(8,128)(2,1)S(1)}) fusion(f32[880,384]{1,0:T(8,128)} %copy-done.20, f32[880,384]{1,0:T(8,128)} %get-tuple-element.36, bf16[880,2048]{1,0:T(8,128)(2,1)} %reshape.102, bf16[1,2048,384]{2,1,0:T(8,128)(2,1)} %param.12), kind=kOutput, calls=%fused_computation.51 | convolution fusion | flops 1388513280 | bytes 9232384 | tf_op jit(solution)/shard_map/dot_general | solution.py:27
  329.1 2.3 convolution_bitcast_fusion.4
  331.4 2.3 convolution_bitcast_fusion.5
  333.7 4.1 pad_maximum_fusion
  337.9 3.8 fusion.23
  341.7 4.0 add_convert_fusion
  345.7 3.9 reshape.103
  349.5 4.8 all-to-all-start.3
  354.5 2.5 fusion.15
  357.0 0.8 fusion.40
  358.4 2.1 fusion.13
  360.5 1.7 select_reduce_fusion
  362.9 10.3 %fusion.8 = bf16[256,2048]{1,0:T(8,128)(2,1)} fusion(f32[880,256]{1,0:T(8,128)S(1)} %convert_reduce_fusion, f32[880,2048]{1,0:T(8,128)} %reshape.105, f32[880]{0:T(1024)S(1)} %fusion.27, bf16[256,2048]{1,0:T(8,128)(2,1)S(1)} %get-tuple-element.38, f32[256]{0:T(256)S(1)} %get-tuple-element.23), kind=kOutput, calls=%fused_computation.29 | convolution fusion | flops 5540380672 | bytes 10211776 | tf_op jit(solution)/shard_map/dot_general | solution.py:89
  373.2 24.6 %all-to-all-done.3 = bf16[8,110,2048]{2,1,0:T(8,128)(2,1)} async-done(((bf16[8,110,2048]{2,1,0:T(8,128)(2,1)}), bf16[8,110,2048]{2,1,0:T(8,128)(2,1)}, u32[]{:S(2)}, u32[]{:S(2)}) %all-to-all-start.3) | async-done | bytes 3604512 | tf_op jit(solution)/shard_map/all_to_all | solution.py:119
  397.9 3.8 reshape.104
  401.7 5.2 %fusion.11 = bf16[256,2048]{1,0:T(8,128)(2,1)} fusion(f32[256,2048]{1,0:T(8,128)} %fusion.13, bf16[880,2048]{1,0:T(8,128)(2,1)} %reshape.104, f32[880,256]{1,0:T(8,128)S(1)} %convert_reduce_fusion), kind=kOutput, calls=%fused_computation.31 | convolution fusion | flops 924020736 | bytes 7651328 | tf_op jit(solution)/shard_map/dot_general | solution.py:122
  406.9 90.7 %reduce-scatter.3.cloned.1.call-done = f32[3,512,384]{2,1,0:T(8,128)} async-done(((f32[3,2048,384]{2,1,0:T(8,128)}), f32[3,512,384]{2,1,0:T(8,128)}) %reduce-scatter.3.cloned.1.call-update) | async-done | bytes 2359312 | tf_op jit(solution)/shard_map/reduce_scatter | solution.py:133
  497.6 2.3 select_add_fusion
  499.9 1.4 fusion.39
  (75 shorter events, 7.9 us)
Async XLA Ops:
  8.0 97.3 %copy-start = (bf16[256,2048]{1,0:T(8,128)(2,1)S(1)}, bf16[256,2048]{1,0:T(8,128)(2,1)}, u32[]{:S(2)}) copy-start(bf16[256,2048]{1,0:T(8,128)(2,1)} %param.7) | copy-start | bytes 3145732
  8.0 5.3 %copy-start.3 = (bf16[1,2048,384]{2,1,0:T(8,128)(2,1)S(1)}, bf16[1,2048,384]{2,1,0:T(8,128)(2,1)}, u32[]{:S(2)}) copy-start(bf16[1,2048,384]{2,1,0:T(8,128)(2,1)} %param.10) | copy-start | bytes 4718596
  8.0 97.3 %all-reduce.3.cloned.1.call-start = ((), (), s32[]{:S(2)}) async-start(), calls=%async_computation.9 | async-start | bytes 9437184 | tf_op jit(solution)/shard_map/psum | solution.py:13
  10.3 2.9 copy-start.4
  15.2 0.7 copy-start.18
  15.2 4.1 copy-start.19
  15.3 306.1 %reduce-scatter.5.cloned.1.call-start = ((), (), s32[]{:S(2)}) async-start(), calls=%async_computation.7 | async-start | bytes 9732096 | tf_op jit(solution)/shard_map/reduce_scatter | solution.py:134
  105.3 2.2 copy-start.12
  107.5 1.2 copy-start.2
  107.5 1.7 copy-start.10
  110.2 0.9 copy-start.15
  176.4 4.7 copy-start.5
  176.4 4.7 copy-start.7
  181.1 3.2 copy-start.20
  181.1 3.2 copy-start.11
  192.0 55.1 %all-to-all-start.1 = ((bf16[8,110,2048]{2,1,0:T(8,128)(2,1)}), bf16[8,110,2048]{2,1,0:T(8,128)(2,1)}, u32[]{:S(2)}, u32[]{:S(2)}) async-start(bf16[8,110,2048]{2,1,0:T(8,128)(2,1)} %reshape.100), calls=%async_computation.1 | async-start | bytes 7340032 | tf_op jit(solution)/shard_map/all_to_all | solution.py:85
  196.5 210.4 %all-gather.2.cloned.1.call-start = ((), (), s32[]{:S(2)}) async-start(), calls=%async_computation.8 | async-start | bytes 1327104 | tf_op jit(solution)/shard_map/all_gather | solution.py:135
  323.0 174.6 %reduce-scatter.3.cloned.1.call-start = ((), (), s32[]{:S(2)}) async-start(), calls=%async_computation.6 | async-start | bytes 11796480 | tf_op jit(solution)/shard_map/reduce_scatter | solution.py:133
  323.3 5.8 %copy-start.8 = (bf16[880,2048]{1,0:T(8,128)(2,1)S(1)}, bf16[880,2048]{1,0:T(8,128)(2,1)}, u32[]{:S(2)}) copy-start(bf16[880,2048]{1,0:T(8,128)(2,1)} %reshape.99) | copy-start | bytes 10813444
  329.0 2.3 copy-start.16
  331.4 2.3 copy-start.9
  337.9 3.8 copy-start.6
  337.9 3.8 copy-start.17
  349.5 48.3 %all-to-all-start.3 = ((bf16[8,110,2048]{2,1,0:T(8,128)(2,1)}), bf16[8,110,2048]{2,1,0:T(8,128)(2,1)}, u32[]{:S(2)}, u32[]{:S(2)}) async-start(bf16[8,110,2048]{2,1,0:T(8,128)(2,1)} %reshape.103), calls=%async_computation.3 | async-start | bytes 7340032 | tf_op jit(solution)/shard_map/all_to_all | solution.py:119
  354.5 2.5 copy-start.14
  357.0 1.4 copy-start.13
  497.6 3.8 copy-start.1
Sparse Core Ops, SparseCore 0:
  15.4 89.9 all-reduce.2
  116.9 159.8 reduce-scatter.4
  323.1 22.5 all-gather.1
Sparse Core Ops, SparseCore 1:
  338.0 159.6 reduce-scatter.2
where the time goes:
time: 516 us; the launch traced here: 509 us
  waiting for transfers between devices  249 us (48%)
  blocking collectives  98.1 us (19%)
  matrix products  73.5 us (14%)
  local copies, waits for them, and re-layouts  37.2 us (7%)
  other arithmetic  24.8 us (5%)
  between operations  16.7 us (3%)
  starting transfers between devices  9.68 us (2%)
    reduce_scatter x1, waiting for transfers between devices, per_device(): own_sum = lax.psum_scatter(own_part, 'dp', scatter_dimension=1, tiled=True)  90.7 us
    psum x1, waiting for transfers between devices, broadcast(): return lax.psum(kept, axis)  85.3 us
    all_to_all x1, blocking collectives, per_device(): lax.all_to_all(outgoing_grad.reshape(experts, capacity, D), 'expert', spl...  49.6 us
    all_to_all x1, blocking collectives, per_device(): lax.all_to_all(outgoing, 'expert', split_axis=0, concat_axis=0, tiled=True)  48.5 us
    all_to_all x1, waiting for transfers between devices, per_device(): lax.all_to_all(expert_out, 'expert', split_axis=0, concat_axis=0, tiled=T...  48.2 us
    all_to_all x1, waiting for transfers between devices, per_device(): lax.all_to_all(input_rows.reshape(experts, capacity, D), 'expert', split_...  24.6 us
    dot_general x1, matrix products, per_device(): lax.dot_general(per_token_f, weighted, over_rows, precision=highest, pref...  10.3 us
  transfers between devices with their start and end apart: 6, of which 4 were waited for; matrix products, arithmetic and copies ran while one was open for 22% of the time, Pallas kernels for 0%

commit v1 on v0

v1 whole, which is shorter than its diff:
```python
import jax
import jax.numpy as jnp
from jax import lax
from jax.experimental import pallas as pl
from jax.experimental.pallas import tpu as pltpu
from jax.sharding import PartitionSpec as P

BF = jnp.bfloat16
F32 = jnp.float32
OVER_ROWS = (((0,), (0,)), ((), ()))
OVER_COLS = (((1,), (1,)), ((), ()))


def add(left, right):
    return (left.astype(F32) + right.astype(F32)).astype(BF)


def join(*values):
    return jnp.concatenate(values, axis=0)


def ends_round(*values):
    return lax.optimization_barrier(values)


def chip_bits():
    return [1 << b for b in range(1, lax.axis_size("expert").bit_length() - 1)]


def flip(value, bit_even, bit_odd):
    size = lax.axis_size("expert")
    pairs = [(i, i ^ (bit_odd if i & 1 else bit_even)) for i in range(size)]
    return lax.ppermute(value, "expert", pairs)


def swap_core(value):
    return flip(value, 1, 1)


def hop(value, step):
    bits = chip_bits()
    return flip(value, bits[step], bits[-1 - step])


def take(stacked, index):
    return lax.dynamic_index_in_dim(stacked, index, 0, keepdims=False)


class LineSum:
    def __init__(self, part):
        self.part = part
        self.size = lax.axis_size("dp")
        self.right, self.left = None, None

    def block(self, index):
        width = self.part.shape[1] // self.size
        start = jnp.clip(index, 0, self.size - 1) * width
        return lax.dynamic_slice_in_dim(self.part, start, width, 1)

    def sends(self, step):
        size, me = self.size, lax.axis_index("dp")
        right, left = self.block(size - step + me), self.block(me - (size - step))
        if step > 1:
            right, left = add(right, self.right), add(left, self.left)
        return right, left

    def send(self, step, right, left):
        size = self.size
        self.right = lax.ppermute(right, "dp", [(i, i + 1) for i in range(step)])
        self.left = lax.ppermute(left, "dp", [(size - 1 - i, size - 2 - i) for i in range(step)])

def line_gather(mine):
    groups = lax.axis_size("dp")
    group = lax.axis_index("dp")
    found = mine[None]
    bit = 1
    while bit < groups:
        found = join(found, lax.ppermute(found, "dp", [(i, i ^ bit) for i in range(groups)]))
        bit *= 2
    return jnp.concatenate([take(found, group ^ j) for j in range(groups)], axis=1)


def row_order():
    lists = []
    for bits in (chip_bits(), chip_bits()[::-1]):
        held = [0]
        for bit in bits:
            held = held + [r ^ bit for r in held]
        lists.append(held)
    half = len(lists[0]) // 2
    orders = []
    for core in (0, 1):
        own, other = lists[core], [r ^ 1 for r in lists[1 - core]]
        orders.append(own[:half] + other[:half] + own[half:] + other[half:])
    return orders


def tile_of(rows):
    tile = min(rows, 256)
    assert rows % tile == 0
    return tile


def call(body, grid, in_specs, out_specs, out_shape):
    return pl.pallas_call(
        body,
        grid=grid,
        in_specs=in_specs,
        out_specs=out_specs,
        out_shape=out_shape,
        cost_estimate=pl.CostEstimate(flops=1000, bytes_accessed=1000, transcendentals=0),
        compiler_params=pltpu.CompilerParams(
            dimension_semantics=("arbitrary",), vmem_limit_bytes=48 * 1024 * 1024
        ),
    )


def by_rows(tile, width):
    return pl.BlockSpec((tile, width), lambda i: (i, 0))


def by_columns(height, tile):
    return pl.BlockSpec((height, tile), lambda i: (0, i))


def whole(shape):
    return pl.BlockSpec(shape, lambda i: (0, 0))


def row_weights(gate_ref, units, shape):
    lane = lax.broadcasted_iota(jnp.int32, shape, 1)
    return jnp.where(lane < units, gate_ref[:, 0:1], gate_ref[:, 1:2])


def first_rows(tile, width, tiles):
    return pl.BlockSpec((tile, width), lambda i: (jnp.minimum(i, tiles - 1), 0))


def second_rows(tile, width, tiles):
    return pl.BlockSpec((tile, width), lambda i: (jnp.maximum(i - tiles, 0), 0))


def on_both(tiles, run, first, second):
    pl.when(pl.program_id(0) < tiles)(lambda: run(*first))
    pl.when(pl.program_id(0) >= tiles)(lambda: run(*second))


def forward(first, second, gate, w_in, w_out, units):
    half, width = first.shape
    count = 2 * half
    hidden_width = w_out.shape[1]
    tile = tile_of(half)
    tiles = half // tile

    def body(a_ref, b_ref, g_ref, wi_ref, wo_ref, act_ref, hidden_ref, out_a_ref, out_b_ref):
        def run(x_ref, out_ref):
            act = jnp.dot(x_ref[...], wi_ref[...], preferred_element_type=F32)
            act_ref[...] = act
            gate_act, up_act = act[:, :hidden_width], act[:, hidden_width:]
            weight = row_weights(g_ref, units, gate_act.shape)
            hidden = (gate_act * jax.nn.sigmoid(gate_act) * up_act * weight).astype(BF)
            hidden_ref[...] = hidden.T
            out_ref[...] = lax.dot_general(
                hidden, wo_ref[...], OVER_COLS, preferred_element_type=F32
            ).astype(BF)

        on_both(tiles, run, (a_ref, out_a_ref), (b_ref, out_b_ref))

    return call(
        body,
        (2 * tiles,),
        [
            first_rows(tile, width, tiles), second_rows(tile, width, tiles), by_rows(tile, 2),
            whole(w_in.shape), whole(w_out.shape),
        ],
        [
            by_rows(tile, 2 * hidden_width), by_columns(hidden_width, tile),
            first_rows(tile, width, tiles), second_rows(tile, width, tiles),
        ],
        [
            jax.ShapeDtypeStruct((count, 2 * hidden_width), F32),
            jax.ShapeDtypeStruct((hidden_width, count), BF),
            jax.ShapeDtypeStruct((half, width), BF),
            jax.ShapeDtypeStruct((half, width), BF),
        ],
    )(first, second, gate, w_in, w_out)


def backward(first, second, act, gate, w_in, w_out, units):
    half, width = first.shape
    count = 2 * half
    hidden_width = w_out.shape[1]
    tile = tile_of(half)
    tiles = half // tile

    def body(a_ref, b_ref, act_ref, g_ref, wi_ref, wo_ref, pre_ref, out_a_ref, out_b_ref, dots_ref):
        def run(c_ref, out_ref):
            raw = jnp.dot(c_ref[...], wo_ref[...], preferred_element_type=F32)
            gate_act, up_act = act_ref[:, :hidden_width], act_ref[:, hidden_width:]
            sigma = jax.nn.sigmoid(gate_act)
            silu = gate_act * sigma
            product = silu * up_act * raw
            lane = lax.broadcasted_iota(jnp.int32, product.shape, 1)
            own = jnp.sum(jnp.where(lane < units, product, 0.0), axis=1, keepdims=True)
            hot = jnp.sum(jnp.where(lane < units, 0.0, product), axis=1, keepdims=True)
            lane = lax.broadcasted_iota(jnp.int32, dots_ref.shape, 1)
            dots_ref[...] = jnp.where(lane == 0, own, hot)
            grad = raw * row_weights(g_ref, units, raw.shape)
            gate_pre = (grad * up_act * sigma * (1.0 + gate_act * (1.0 - sigma))).astype(BF)
            up_pre = (grad * silu).astype(BF)
            pre_ref[:hidden_width, :] = gate_pre.T
            pre_ref[hidden_width:, :] = up_pre.T
            pre = jnp.concatenate([gate_pre, up_pre], axis=1)
            out_ref[...] = lax.dot_general(
                pre, wi_ref[...], OVER_COLS, preferred_element_type=F32
            ).astype(BF)

        on_both(tiles, run, (a_ref, out_a_ref), (b_ref, out_b_ref))

    return call(
        body,
        (2 * tiles,),
        [
            first_rows(tile, width, tiles), second_rows(tile, width, tiles),
            by_rows(tile, 2 * hidden_width), by_rows(tile, 2), whole(w_in.shape), whole(w_out.shape),
        ],
        [
            by_columns(2 * hidden_width, tile), first_rows(tile, width, tiles),
            second_rows(tile, width, tiles), by_rows(tile, 2),
        ],
        [
            jax.ShapeDtypeStruct((2 * hidden_width, count), BF),
            jax.ShapeDtypeStruct((half, width), BF),
            jax.ShapeDtypeStruct((half, width), BF),
            jax.ShapeDtypeStruct((count, 2), F32),
        ],
    )(first, second, act, gate, w_in, w_out)


def weight_sums(pre, xs, hidden, cs):
    half, width = xs[0].shape
    tile = min(width, 512)

    def body(pre_ref, xa_ref, xb_ref, hidden_ref, ca_ref, cb_ref, in_ref, down_ref):
        in_ref[...] = both(pre_ref, xa_ref, xb_ref)
        down_ref[...] = both(hidden_ref, ca_ref, cb_ref)

    cut = by_columns(half, tile)
    return call(
        body,
        (width // tile,),
        [whole(pre.shape), cut, cut, whole(hidden.shape), cut, cut],
        [by_columns(pre.shape[0], tile), by_columns(hidden.shape[0], tile)],
        [
            jax.ShapeDtypeStruct((pre.shape[0], width), F32),
            jax.ShapeDtypeStruct((hidden.shape[0], width), F32),
        ],
    )(pre, *xs, hidden, *cs)


def both(left_ref, a_ref, b_ref):
    half = a_ref.shape[0]
    value = jnp.dot(left_ref[:, :half], a_ref[...], preferred_element_type=F32)
    return value + jnp.dot(left_ref[:, half:], b_ref[...], preferred_element_type=F32)


def weight_totals(pre, xs, hidden, cs, in_sum, down_sum, units):
    half, width = xs[0].shape
    tile = min(width, 512)
    padded = hidden.shape[0]
    spare = padded - units

    def body(pre_ref, xa_ref, xb_ref, hidden_ref, ca_ref, cb_ref, in_ref, down_ref, own_ref, hot_ref):
        total = in_ref[...] + both(pre_ref, xa_ref, xb_ref)
        own_ref[:units, :] = total[:units].astype(BF)
        own_ref[units : 2 * units, :] = total[padded : padded + units].astype(BF)
        hot_ref[:spare, :] = total[units:padded].astype(BF)
        hot_ref[spare : 2 * spare, :] = total[padded + units :].astype(BF)
        total = down_ref[...] + both(hidden_ref, ca_ref, cb_ref)
        own_ref[2 * units :, :] = total[:units].astype(BF)
        hot_ref[2 * spare :, :] = total[units:].astype(BF)

    cut = by_columns(half, tile)
    return call(
        body,
        (width // tile,),
        [
            whole(pre.shape), cut, cut, whole(hidden.shape), cut, cut,
            by_columns(2 * padded, tile), by_columns(padded, tile),
        ],
        [by_columns(3 * units, tile), by_columns(3 * spare, tile)],
        [
            jax.ShapeDtypeStruct((3 * units, width), BF),
            jax.ShapeDtypeStruct((3 * spare, width), BF),
        ],
    )(pre, *xs, hidden, *cs, in_sum, down_sum)


def sum_of(*arrays):
    rows, width = arrays[0].shape
    tile = min(rows, 128)

    def body(*refs):
        total = refs[0][...].astype(F32)
        for ref in refs[1:-1]:
            total = total + ref[...].astype(F32)
        refs[-1][...] = total.astype(BF)

    return call(
        body,
        (rows // tile,),
        [by_rows(tile, width)] * len(arrays),
        by_rows(tile, width),
        jax.ShapeDtypeStruct((rows, width), BF),
    )(*arrays)


def halves_of_sum(*arrays):
    half, width = arrays[0].shape[0] // 2, arrays[0].shape[1]
    tile = min(half, 128)
    tiles = half // tile

    def body(*refs):
        def run(out_ref):
            total = refs[0][...].astype(F32)
            for ref in refs[1:-2]:
                total = total + ref[...].astype(F32)
            out_ref[...] = total.astype(BF)

        on_both(tiles, run, (refs[-2],), (refs[-1],))

    shape = jax.ShapeDtypeStruct((half, width), BF)
    return call(
        body,
        (2 * tiles,),
        [by_rows(tile, width)] * len(arrays),
        [first_rows(tile, width, tiles), second_rows(tile, width, tiles)],
        [shape, shape],
    )(*arrays)


def fold(*arrays):
    for step in range(len(chip_bits()) - 2, -1, -1):
        mine, other = halves_of_sum(*arrays)
        arrays = (mine, hop(other, step))
    return sum_of(*arrays)


def finish(mine, right, left, hot, is_owner):
    units, width = hot.shape[1:]

    def body(flag_ref, mine_ref, right_ref, left_ref, hot_ref, out_ref):
        total = mine_ref[...].astype(F32) + right_ref[...].astype(F32) + left_ref[...].astype(F32)
        total = jnp.where(flag_ref[0] > 0, hot_ref[0].astype(F32), total)
        out_ref[0] = total.T

    block = pl.BlockSpec((units, width), lambda i: (i, 0))
    return pl.pallas_call(
        body,
        grid=(3,),
        in_specs=[
            pl.BlockSpec(memory_space=pltpu.SMEM), block, block, block,
            pl.BlockSpec((1, units, width), lambda i: (i, 0, 0)),
        ],
        out_specs=pl.BlockSpec((1, width, units), lambda i: (i, 0, 0)),
        out_shape=jax.ShapeDtypeStruct((3, width, units), F32),
        compiler_params=pltpu.CompilerParams(vmem_limit_bytes=32 * 1024 * 1024),
    )(is_owner.astype(jnp.int32).reshape(1), mine, right, left, hot)


def hot_pieces(weights, is_owner):
    experts, groups = lax.axis_size("expert"), lax.axis_size("dp")
    width, units = weights[0].shape
    part = width // groups
    start = lax.axis_index("dp") * part
    pieces = [
        lax.dynamic_slice_in_dim(w, start, part, 0).T.reshape(experts, units // experts, part)
        for w in weights
    ]
    pieces = jnp.concatenate(pieces, axis=1)
    return jnp.where(is_owner, pieces, jnp.zeros_like(pieces))


def per_device(tokens, expert_ids, gates, w_gate, w_up, w_down, cotangent):
    experts, groups = lax.axis_size("expert"), lax.axis_size("dp")
    me, group = lax.axis_index("expert"), lax.axis_index("dp")
    tok_rows, width = tokens.shape
    units = w_gate.shape[2]
    share = units // experts
    last = len(chip_bits()) - 1
    expert_range = jnp.arange(experts, dtype=jnp.int32)
    matches = expert_ids[:, :, None] == expert_range
    hot_expert = jnp.argmax(jnp.sum(matches.astype(jnp.int32), axis=(0, 1))).astype(jnp.int32)
    is_owner = me == hot_expert
    is_me = ((expert_range == me) & ~is_owner)[:, None]
    is_hot = (expert_range == hot_expert)[:, None]
    routed = jnp.sum(jnp.where(matches, gates[:, :, None], 0.0), axis=1).T
    own = (w_gate[0], w_up[0], w_down[0])
    orders = row_order()
    x_held, c_held, r_held = tokens, cotangent, routed
    for step in range(last):
        x_held = join(x_held, hop(x_held, step))
        c_held = join(c_held, hop(c_held, step))
        r_held = jnp.concatenate([r_held, hop(r_held, step)], axis=1)
    r_last = hop(r_held, last)
    hot = hot_pieces(own, is_owner)
    bit = 1
    while bit < experts:
        hot = hot.reshape((hot.shape[0] // 2, 2) + hot.shape[1:])
        mark = (me // bit) % 2
        other = lax.dynamic_index_in_dim(hot, 1 - mark, 1, keepdims=False)
        hot = lax.dynamic_index_in_dim(hot, mark, 1, keepdims=False)
        hot = hot + flip(other, bit, bit)
        bit *= 2
    hot = hot[0]
    x_held, c_held, r_held, r_last, hot = ends_round(x_held, c_held, r_held, r_last, hot)

    x_last, c_last = hop(x_held, last), hop(c_held, last)
    x_other, c_other = swap_core(x_held), swap_core(c_held)
    r_held = jnp.concatenate([r_held, r_last], axis=1)
    r_other = swap_core(r_held)
    half = x_held.shape[0]
    own_gate, hot_gate = (
        [jnp.sum(jnp.where(mask, table, 0.0), axis=0) for table in (r_held, r_other)]
        for mask in (is_me, is_hot)
    )

    def gates_of(part):
        columns = [
            jnp.concatenate([value[part] for value in values]) for values in (own_gate, hot_gate)
        ]
        return jnp.stack(columns).T

    gate_near, gate_far = gates_of(slice(None, half)), gates_of(slice(half, None))
    spare = share + -(units + share) % 128
    hot = line_gather(hot).reshape(3, share, width)
    hot = jnp.pad(hot, ((0, 0), (0, spare - share), (0, 0))).reshape(3 * spare, width).T
    w_in = jnp.concatenate([own[0], hot[:, :spare], own[1], hot[:, spare : 2 * spare]], axis=1)
    w_out = jnp.concatenate([own[2], hot[:, 2 * spare :]], axis=1)
    a_near, s_near, m_near, m_near_far = forward(x_held, x_other, gate_near, w_in, w_out, units)
    p_near, t_near, t_near_far, d_near = backward(
        c_held, c_other, a_near, gate_near, w_in, w_out, units
    )
    (
        x_last, c_last, m_near, m_near_far, t_near, t_near_far, d_near, gate_far,
        w_in, w_out, p_near, s_near, x_held, x_other, c_held, c_other,
    ) = ends_round(
        x_last, c_last, m_near, m_near_far, t_near, t_near_far, d_near, gate_far,
        w_in, w_out, p_near, s_near, x_held, x_other, c_held, c_other,
    )

    x_last_other, c_last_other = swap_core(x_last), swap_core(c_last)
    in_near, down_near = weight_sums(p_near, (x_held, x_other), s_near, (c_held, c_other))
    x_last, x_last_other, c_last, c_last_other, m_near, m_near_far, t_near, t_near_far, in_near, down_near = (
        ends_round(
            x_last, x_last_other, c_last, c_last_other, m_near, m_near_far, t_near, t_near_far,
            in_near, down_near,
        )
    )

    m_near_other, t_near_other = swap_core(m_near_far), swap_core(t_near_far)
    a_far, s_far, m_far, m_far_far = forward(x_last, x_last_other, gate_far, w_in, w_out, units)
    m_far_other = swap_core(m_far_far)
    p_far, t_far, t_far_far, d_far = backward(
        c_last, c_last_other, a_far, gate_far, w_in, w_out, units
    )
    own_grad, hot_grad = weight_totals(
        p_far, (x_last, x_last_other), s_far, (c_last, c_last_other), in_near, down_near, units
    )
    line = LineSum(own_grad)
    right, left = line.sends(1)
    right, left, m_far, m_far_other, t_far, t_far_far, d_far, hot_grad, m_near, m_near_other = ends_round(
        right, left, m_far, m_far_other, t_far, t_far_far, d_far, hot_grad, m_near, m_near_other
    )

    line.send(1, right, left)
    m_got = hop(sum_of(m_far, m_far_other), last)
    t_far_other = swap_core(t_far_far)
    hot_grad = hot_grad.reshape(3, spare, width)[:, :share].reshape(3 * share, width)
    hot_sum = lax.psum_scatter(hot_grad, "dp", scatter_dimension=1, tiled=True)
    t_far, t_far_other, m_got, line.right, line.left = ends_round(
        t_far, t_far_other, m_got, line.right, line.left
    )

    right, left = line.sends(2)
    right, left, t_far, t_far_other, m_got, m_near, m_near_other = ends_round(
        right, left, t_far, t_far_other, m_got, m_near, m_near_other
    )
    line.send(2, right, left)
    t_got = hop(sum_of(t_far, t_far_other), last)
    mixed = fold(m_near, m_near_other, m_got)
    dots = lax.all_gather(jnp.concatenate([d_near, d_far]).T, "expert", axis=0)
    mixed, t_got, dots, hot_sum, line.right, line.left = ends_round(
        mixed, t_got, dots, hot_sum, line.right, line.left
    )

    for step in range(3, groups):
        right, left = line.sends(step)
        right, left, t_near, t_near_other, t_got = ends_round(right, left, t_near, t_near_other, t_got)
        line.send(step, right, left)
    tokens_grad = fold(t_near, t_near_other, t_got)
    hot_all = lax.all_gather(hot_sum.astype(BF), "expert", axis=0)

    my_dots = []
    for source in range(experts):
        order = orders[source % 2]
        place = jnp.array([order.index(r) for r in range(experts)], jnp.int32)
        place = jnp.sum(jnp.where(expert_range == (me ^ source), place, 0))
        my_dots.append(lax.dynamic_slice_in_dim(dots[source], place * tok_rows, tok_rows, 1))
    my_dots = jnp.stack(my_dots)
    hot_dot = jnp.sum(my_dots[:, 1], axis=0)
    own_dot = jnp.sum(jnp.where(matches, my_dots[:, 0].T[:, None, :], 0.0), axis=2)
    gates_grad = jnp.where(expert_ids == hot_expert, hot_dot[:, None], own_dot)

    hot_all = hot_all.reshape(experts, 3, share, width // groups)
    hot_all = jnp.moveaxis(hot_all, 1, 0).reshape(3, units, width // groups)
    grads = finish(line.block(group), line.right, line.left, hot_all, is_owner)
    return (mixed, tokens_grad, gates_grad, grads[0:1], grads[1:2], grads[2:3])


def solution(mesh):
    rows = P(("dp", "expert"), None)
    weight = P("expert", None, None)
    grad = P("expert", "dp", None)
    return jax.shard_map(
        per_device,
        mesh=mesh,
        in_specs=(rows, rows, rows, weight, weight, weight, rows),
        out_specs=(rows, rows, rows, grad, grad, grad),
        check_vma=False,
    )
```

time: 516 us -> 319 us (0.62); the launches traced: 509 us -> 318 us
  waiting for transfers between devices: 249 us -> 80.9 us
  Pallas kernels: 0 us -> 93 us
  blocking collectives: 98.1 us -> 16.6 us
  matrix products: 73.5 us -> 0 us
  starting transfers between devices: 9.68 us -> 43.8 us
    all_to_all x2 -> x0, blocking collectives: 98.1 us -> none  [the longest x1 49.6 us: per_device(): lax.all_to_all(outgoing_grad.reshape(experts, capacity, D), 'expert', spl...]
    pallas_call x0 -> x13, Pallas kernels: none -> 93 us  [the longest x2 26.6 us: backward(): call(body, (2 * tiles,), [first_rows(tile, width, tiles), second_rows(til...]
    reduce_scatter x2 -> x1, waiting for transfers between devices: 90.7 us -> 0.01 us  [per_device(): hot_sum = lax.psum_scatter(hot_grad, 'dp', scatter_dimension=1, tiled=True)]
    psum x1 -> x0, waiting for transfers between devices: 85.3 us -> none  [broadcast(): return lax.psum(kept, axis)]
    ppermute x0 -> x30, waiting for transfers between devices: none -> 80.9 us  [the longest x3 34.3 us: send(): self.right = lax.ppermute(right, 'dp', [(i, i + 1) for i in range(step)])]
    dot_general x23 -> x0, matrix products: 73.5 us -> none  [the longest x1 10.3 us: per_device(): lax.dot_general(per_token_f, weighted, over_rows, precision=highest, pref...]
    all_to_all x2 -> x0, waiting for transfers between devices: 72.8 us -> none  [the longest x1 48.2 us: per_device(): lax.all_to_all(expert_out, 'expert', split_axis=0, concat_axis=0, tiled=T...]
    ppermute x0 -> x30, starting transfers between devices: none -> 43.8 us  [the longest x3 18.2 us: send(): self.right = lax.ppermute(right, 'dp', [(i, i + 1) for i in range(step)])]
  transfers between devices with their start and end apart: 6 -> 32, of which waited for: 4 -> 11; matrix products, arithmetic and copies ran while one was open for 22% -> 13% of each run, Pallas kernels for 0% -> 27%
where the time goes in v1:
time: 319 us; the launch traced here: 318 us
  Pallas kernels  93 us (29%)
  waiting for transfers between devices  80.9 us (25%)
  starting transfers between devices  43.8 us (14%)
  local copies, waits for them, and re-layouts  35.6 us (11%)
  other arithmetic  27.9 us (9%)
  between operations  20.2 us (6%)
  blocking collectives  16.6 us (5%)
    ppermute x3, waiting for transfers between devices, send(): self.right = lax.ppermute(right, 'dp', [(i, i + 1) for i in range(step)])  34.3 us
    pallas_call x2, Pallas kernels, backward(): call(body, (2 * tiles,), [first_rows(tile, width, tiles), second_rows(til...  26.6 us
    pallas_call x2, Pallas kernels, forward(): call(body, (2 * tiles,), [first_rows(tile, width, tiles), second_rows(til...  25.2 us
    ppermute x22, waiting for transfers between devices, flip(): return lax.ppermute(value, 'expert', pairs)  25 us
    ppermute x3, starting transfers between devices, send(): self.right = lax.ppermute(right, 'dp', [(i, i + 1) for i in range(step)])  18.2 us
    ppermute x2, waiting for transfers between devices, line_gather(): lax.ppermute(found, 'dp', [(i, i ^ bit) for i in range(groups)])  17.5 us
    ppermute x22, starting transfers between devices, flip(): return lax.ppermute(value, 'expert', pairs)  16.7 us
    all_gather x1, blocking collectives, per_device(): dots = lax.all_gather(jnp.concatenate([d_near, d_far]).T, 'expert', axis=0)  16.6 us
  transfers between devices with their start and end apart: 32, of which 11 were waited for; matrix products, arithmetic and copies ran while one was open for 13% of the time, Pallas kernels for 27%

profile of v1, /device:TPU:0, one launch (start us, length us, event | category | flops | bytes accessed | tf_op | source)
XLA Modules:
  0.0 318.0 jit_solution(14352884664628563830)
XLA Ops:
  13.0 1.8 collective-permute-done.4
  15.9 2.9 collective-permute-start.5
  18.9 2.0 collective-permute-start.2
  21.0 5.1 %collective-permute-done.5 = bf16[2,144,512]{2,1,0:T(8,128)(2,1)S(1)} collective-permute-done((bf16[2,144,512]{2,1,0:T(8,128)(2,1)S(1)}, bf16[2,144,512]{2,1,0:T(8,128)(2,1)S(1)}, u32[]{:S(2)}, u32[]{:S(2)}) %collective-permute-start.5) | collective-permute-done | bytes 294944 | tf_op jit(solution)/shard_map/ppermute | solution.py:33
  26.2 1.8 collective-permute-start.6
  28.6 9.0 %collective-permute-done.2 = f32[8,256]{1,0:T(8,128)S(1)} collective-permute-done((f32[8,256]{1,0:T(8,128)S(1)}, f32[8,256]{1,0:T(8,128)S(1)}, u32[]{:S(2)}, u32[]{:S(2)}) %collective-permute-start.2) | collective-permute-done | bytes 8224 | tf_op jit(solution)/shard_map/ppermute | solution.py:33
  37.6 1.8 collective-permute-start.3
  39.5 1.5 pad_maximum_fusion.1.a_ref.xa_ref
  41.0 8.0 %collective-permute-done.1 = bf16[256,2048]{1,0:T(8,128)(2,1)} collective-permute-done((bf16[256,2048]{1,0:T(8,128)(2,1)}, bf16[256,2048]{1,0:T(8,128)(2,1)}, u32[]{:S(2)}, u32[]{:S(2)}) %collective-permute-start.1) | collective-permute-done | bytes 1048608 | tf_op jit(solution)/shard_map/ppermute | solution.py:33
  49.0 2.9 pad_maximum_fusion.2.a_ref.ca_ref
  52.8 1.5 collective-permute-start.7
  55.5 1.6 collective-permute-start.11
  57.5 4.2 %collective-permute-done.11 = bf16[1,144,512]{2,1,0:T(8,128)(2,1)S(1)} collective-permute-done((bf16[1,144,512]{2,1,0:T(8,128)(2,1)S(1)}, bf16[1,144,512]{2,1,0:T(8,128)(2,1)S(1)}, u32[]{:S(2)}, u32[]{:S(2)}) %collective-permute-start.11) | collective-permute-done | bytes 147488 | tf_op jit(solution)/shard_map/ppermute | solution.py:78
  62.4 2.6 collective-permute-start.12
  65.3 13.3 %collective-permute-done.12 = bf16[2,144,512]{2,1,0:T(8,128)(2,1)} collective-permute-done((bf16[2,144,512]{2,1,0:T(8,128)(2,1)}, bf16[2,144,512]{2,1,0:T(8,128)(2,1)}, u32[]{:S(2)}, u32[]{:S(2)}) %collective-permute-start.12) | collective-permute-done | bytes 294944 | tf_op jit(solution)/shard_map/ppermute | solution.py:78
  81.0 2.6 copy.60
  83.6 1.6 fusion.16
  85.5 1.5 pad_maximum_fusion.3.wo_ref
  88.2 2.3 pad_maximum_fusion.wi_ref
  90.5 12.6 %shard_map.190 = (f32[1024,1024]{1,0:T(8,128)}, bf16[512,1024]{1,0:T(8,128)(2,1)S(1)}, bf16[512,2048]{1,0:T(8,128)(2,1)S(1)}, bf16[512,2048]{1,0:T(8,128)(2,1)}) custom-call(bf16[512,2048]{1,0:T(8,128)(2,1)} %copy-done, bf16[512,2048]{1,0:T(8,128)(2,1)} %collective-permute-done.9.b_ref.xb_ref, f32[1024,2]{1,0:T(8,128)S(1)} %bitcast.61, ...), custom_call_target="tpu_custom_call" | custom-call | flops 1000 | bytes 1000 | tf_op jit(solution)/shard_map/pallas_call | solution.py:169
  104.4 13.4 %shard_map.191 = (bf16[1024,1024]{1,0:T(8,128)(2,1)S(1)}, bf16[512,2048]{1,0:T(8,128)(2,1)S(1)}, bf16[512,2048]{1,0:T(8,128)(2,1)}, f32[1024,2]{1,0:T(8,128)S(1)}) custom-call(bf16[512,2048]{1,0:T(8,128)(2,1)} %pad_maximum_fusion.2.a_ref.ca_ref, bf16[512,2048]{1,0:T(8,128)(2,1)} %collective-permute-done.13.b_ref.cb_ref, ...), custom_call_target="tpu_custom_call" | custom-call | flops 1000 | bytes 1000 | tf_op jit(solution)/shard_map/pallas_call | solution.py:220
  117.7 1.4 copy-done.2
  119.7 9.9 %shard_map.192 = (f32[1024,2048]{1,0:T(8,128)}, f32[512,2048]{1,0:T(8,128)}) custom-call(bf16[1024,1024]{1,0:T(8,128)(2,1)S(1)} %get-tuple-element.115.pre_ref, bf16[512,2048]{1,0:T(8,128)(2,1)S(1)} %copy-done.1, bf16[512,2048]{1,0:T(8,128)(2,1)} %collective-permute-done.9.b_ref.xb_ref, bf16[512,1024]{1,0:T(8,128)(2,1)S(1)} %get-tuple-element.118.hidden_ref, ...), custom_call_target="tpu_custom_call" | custom-call | flops 1000 | bytes 1000 | tf_op jit(solution)/shard_map/pallas_call | solution.py:249
  130.9 12.6 %shard_map.193 = (f32[1024,1024]{1,0:T(8,128)}, bf16[512,1024]{1,0:T(8,128)(2,1)S(1)}, bf16[512,2048]{1,0:T(8,128)(2,1)S(1)}, bf16[512,2048]{1,0:T(8,128)(2,1)}) custom-call(bf16[512,2048]{1,0:T(8,128)(2,1)} %collective-permute-done.7.a_ref.xa_ref, bf16[512,2048]{1,0:T(8,128)(2,1)} %copy-done.17, f32[1024,2]{1,0:T(8,128)S(1)} %bitcast.59, ...), custom_call_target="tpu_custom_call" | custom-call | flops 1000 | bytes 1000 | tf_op jit(solution)/shard_map/pallas_call | solution.py:169
  145.1 13.2 %shard_map.194 = (bf16[1024,1024]{1,0:T(8,128)(2,1)S(1)}, bf16[512,2048]{1,0:T(8,128)(2,1)S(1)}, bf16[512,2048]{1,0:T(8,128)(2,1)}, f32[1024,2]{1,0:T(8,128)S(1)}) custom-call(bf16[512,2048]{1,0:T(8,128)(2,1)} %collective-permute-done.8.a_ref.ca_ref, bf16[512,2048]{1,0:T(8,128)(2,1)} %copy-done.18, f32[1024,1024]{1,0:T(8,128)} %get-tuple-element.130.act_ref, ...), custom_call_target="tpu_custom_call" | custom-call | flops 1000 | bytes 1000 | tf_op jit(solution)/shard_map/pallas_call | solution.py:220
  159.7 12.5 %shard_map.195 = (bf16[1152,2048]{1,0:T(8,128)(2,1)}, bf16[384,2048]{1,0:T(8,128)(2,1)S(1)}) custom-call(bf16[1024,1024]{1,0:T(8,128)(2,1)S(1)} %get-tuple-element.131.pre_ref, bf16[512,2048]{1,0:T(8,128)(2,1)} %collective-permute-done.7.a_ref.xa_ref, bf16[512,2048]{1,0:T(8,128)(2,1)} %copy-done.17, bf16[512,1024]{1,0:T(8,128)(2,1)S(1)} %get-tuple-element.132.hidden_ref, ...), custom_call_target="tpu_custom_call" | custom-call | flops 1000 | bytes 1000 | tf_op jit(solution)/shard_map/pallas_call | solution.py:284
  172.2 4.2 %constant_dynamic-slice_fusion = (bf16[1152,512]{1,0:T(8,128)(2,1)S(1)}, bf16[1152,512]{1,0:T(8,128)(2,1)}, bf16[1152,512]{1,0:T(8,128)(2,1)}) fusion(bf16[1152,2048]{1,0:T(8,128)(2,1)} %get-tuple-element.135, s32[]{:T(128)S(6)} %select_n.217, s32[]{:T(128)S(6)} %select_n.195, s32[]{:T(128)S(6)} %select_n.194), kind=kLoop, calls=%fused_computation.38 | loop fusion | bytes 7077900 | tf_op jit(solution)/shard_map/dynamic_slice | solution.py:58
  176.5 2.6 shard_map.196
  179.5 3.6 %collective-permute-start.20 = (bf16[1152,512]{1,0:T(8,128)(2,1)}, bf16[1152,512]{1,0:T(8,128)(2,1)}, u32[]{:S(2)}, u32[]{:S(2)}) collective-permute-start(bf16[1152,512]{1,0:T(8,128)(2,1)} %get-tuple-element.148), channel_id=1, source_target_pairs={{0,8},{1,9},{2,10},{3,11},{4,12},{5,13},{6,14},{7,15}} | collective-permute-start | bytes 3538952 | tf_op jit(solution)/shard_map/ppermute | solution.py:69
  183.1 1.7 collective-permute-start.21
  184.8 23.2 %collective-permute-done.20 = bf16[1152,512]{1,0:T(8,128)(2,1)} collective-permute-done((bf16[1152,512]{1,0:T(8,128)(2,1)}, bf16[1152,512]{1,0:T(8,128)(2,1)}, u32[]{:S(2)}, u32[]{:S(2)}) %collective-permute-start.20) | collective-permute-done | bytes 1179680 | tf_op jit(solution)/shard_map/ppermute | solution.py:69
  208.0 4.4 %add_convert_fusion.2 = (bf16[1152,512]{1,0:T(8,128)(2,1)}, bf16[1152,512]{1,0:T(8,128)(2,1)}) fusion(bf16[1152,512]{1,0:T(8,128)(2,1)} %collective-permute-done.21, bf16[1152,2048]{1,0:T(8,128)(2,1)} %get-tuple-element.135, s32[]{:T(128)S(6)} %select_n.196, bf16[1152,512]{1,0:T(8,128)(2,1)} %collective-permute-done.20, s32[]{:T(128)S(6)} %select_n.193), kind=kLoop, calls=%fused_computation.8 | loop fusion | flops 4718592 | bytes 7077896 | tf_op jit(solution)/shard_map/convert_element_type | solution.py:15
  212.4 4.1 %shard_map.199 = bf16[512,2048]{1,0:T(8,128)(2,1)} custom-call(bf16[512,2048]{1,0:T(8,128)(2,1)S(1)} %copy-done.7, bf16[512,2048]{1,0:T(8,128)(2,1)} %collective-permute-done.18.refs_1_), custom_call_target="tpu_custom_call" | custom-call | flops 1000 | bytes 1000 | tf_op jit(solution)/shard_map/pallas_call | solution.py:309
  216.5 1.9 collective-permute-start.23
  218.4 1.9 slice.103
  220.4 5.4 %collective-permute-start.24 = (bf16[1152,512]{1,0:T(8,128)(2,1)}, bf16[1152,512]{1,0:T(8,128)(2,1)}, u32[]{:S(2)}, u32[]{:S(2)}) collective-permute-start(bf16[1152,512]{1,0:T(8,128)(2,1)} %get-tuple-element.167), channel_id=1, source_target_pairs={{0,8},{8,16},{1,9},{9,17},{2,10},{10,18},{3,11},{11,19},{4,12},{12... | collective-permute-start | bytes 3538952 | tf_op jit(solution)/shard_map/ppermute | solution.py:69
  225.9 1.7 collective-permute-start.25
  227.6 4.0 %shard_map.197 = (bf16[256,2048]{1,0:T(8,128)(2,1)S(1)}, bf16[256,2048]{1,0:T(8,128)(2,1)}) custom-call(bf16[512,2048]{1,0:T(8,128)(2,1)S(1)} %copy-done.5, bf16[512,2048]{1,0:T(8,128)(2,1)} %collective-permute-done.17.refs_1_, bf16[512,2048]{1,0:T(8,128)(2,1)} %collective-permute-done.19.refs_2_), custom_call_target="tpu_custom_call" | custom-call | flops 1000 | bytes 1000 | tf_op jit(solution)/shard_map/pallas_call | solution.py:333
  241.8 16.6 %all-gather.2 = f32[8,2,2048]{2,1,0:T(2,128)} all-gather(f32[1,2,2048]{2,1,0:T(2,128)S(1)} %maximum_bitcast_fusion), channel_id=2, replica_groups=mesh['dp'=4,'expert'=8] {'expert'}, dimensions={0}, use_global_device_ids=true | all-gather | bytes 147456 | tf_op jit(solution)/shard_map/all_gather | solution.py:492
  260.6 4.6 %add_convert_fusion = (bf16[1152,512]{1,0:T(8,128)(2,1)}, bf16[1152,512]{1,0:T(8,128)(2,1)}) fusion(bf16[1152,512]{1,0:T(8,128)(2,1)} %collective-permute-done.25, bf16[1152,2048]{1,0:T(8,128)(2,1)} %get-tuple-element.135, s32[]{:T(128)S(6)} %select_n.198, bf16[1152,512]{1,0:T(8,128)(2,1)} %collective-permute-done.24, s32[]{:T(128)S(6)} %select_n.197), kind=kLoop, calls=%fused_computation.6 | loop fusion | flops 4718592 | bytes 7077896 | tf_op jit(solution)/shard_map/convert_element_type | solution.py:15
  265.1 4.0 %shard_map.200 = (bf16[256,2048]{1,0:T(8,128)(2,1)S(1)}, bf16[256,2048]{1,0:T(8,128)(2,1)}) custom-call(bf16[512,2048]{1,0:T(8,128)(2,1)S(1)} %copy-done.3, bf16[512,2048]{1,0:T(8,128)(2,1)} %collective-permute-done.26.refs_1_, bf16[512,2048]{1,0:T(8,128)(2,1)} %collective-permute-done.23.refs_2_), custom_call_target="tpu_custom_call" | custom-call | flops 1000 | bytes 1000 | tf_op jit(solution)/shard_map/pallas_call | solution.py:333
  270.4 9.1 %collective-permute-start.28 = (bf16[1152,512]{1,0:T(8,128)(2,1)}, bf16[1152,512]{1,0:T(8,128)(2,1)S(1)}, u32[]{:S(2)}, u32[]{:S(2)}) collective-permute-start(bf16[1152,512]{1,0:T(8,128)(2,1)} %get-tuple-element.181), channel_id=1, source_target_pairs={{0,8},{8,16},{16,24},{1,9},{9,17},{17,25},{2,10},{10,18},{18,26},{... | collective-permute-start | bytes 3538952 | tf_op jit(solution)/shard_map/ppermute | solution.py:69
  287.1 1.8 compare_select_fusion
  291.2 2.1 shard_map.201
  293.4 1.4 copy.72
  294.7 10.1 %collective-permute-done.28.right_ref = bf16[1152,512]{1,0:T(8,128)(2,1)S(1)} collective-permute-done((bf16[1152,512]{1,0:T(8,128)(2,1)}, bf16[1152,512]{1,0:T(8,128)(2,1)S(1)}, u32[]{:S(2)}, u32[]{:S(2)}) %collective-permute-start.28) | collective-permute-done | bytes 1179680 | tf_op jit(solution)/shard_map/ppermute | solution.py:69
  304.8 4.1 %collective-permute-done.29.left_ref = bf16[1152,512]{1,0:T(8,128)(2,1)S(1)} collective-permute-done((bf16[1152,512]{1,0:T(8,128)(2,1)}, bf16[1152,512]{1,0:T(8,128)(2,1)S(1)}, u32[]{:S(2)}, u32[]{:S(2)}) %collective-permute-start.29) | collective-permute-done | bytes 1179680 | tf_op jit(solution)/shard_map/ppermute | solution.py:70
  309.7 1.4 fusion.15
  (165 shorter events, 40.2 us)
Async XLA Ops:
  7.2 252.3 %reduce-scatter.2.cloned.1.call-start = ((), (), s32[]{:S(2)}) async-start(), calls=%async_computation.1 | async-start | bytes 737280 | tf_op jit(solution)/shard_map/reduce_scatter | solution.py:480
  12.3 6.5 %copy-start.22 = (bf16[256,2048]{1,0:T(8,128)(2,1)S(1)}, bf16[256,2048]{1,0:T(8,128)(2,1)}, u32[]{:S(2)}) copy-start(bf16[256,2048]{1,0:T(8,128)(2,1)} %param.15) | copy-start | bytes 3145732
  12.4 6.5 %copy-start.25 = (s32[256,4]{0,1:T(4,128)S(1)}, s32[256,4]{0,1:T(4,128)}, u32[]{:S(2)}) copy-start(s32[256,4]{0,1:T(4,128)} %param.16) | copy-start | bytes 12292
  12.4 6.5 %copy-start.26 = (f32[256,4]{0,1:T(4,128)S(1)}, f32[256,4]{0,1:T(4,128)}, u32[]{:S(2)}) copy-start(f32[256,4]{0,1:T(4,128)} %param.17) | copy-start | bytes 12292
  12.4 2.3 collective-permute-start.4
  15.9 10.2 %collective-permute-start.5 = (bf16[2,144,512]{2,1,0:T(8,128)(2,1)S(1)}, bf16[2,144,512]{2,1,0:T(8,128)(2,1)S(1)}, u32[]{:S(2)}, u32[]{:S(2)}) collective-permute-start(bf16[2,144,512]{2,1,0:T(8,128)(2,1)S(1)} %dynamic-slice_bitcast_fusion.1), channel_id=1, source_target_pairs={{0,2},{1,3},{2,0},{3,1},{4,6},{5,7},{6,4},{7,5},{8,10},{9,11},{10,... | collective-permute-start | bytes 884744 | tf_op jit(solution)/shard_map/ppermute | solution.py:33
  18.8 20.6 %collective-permute-start = (bf16[256,2048]{1,0:T(8,128)(2,1)S(1)}, bf16[256,2048]{1,0:T(8,128)(2,1)}, u32[]{:S(2)}, u32[]{:S(2)}) collective-permute-start(bf16[256,2048]{1,0:T(8,128)(2,1)S(1)} %copy-done.22), channel_id=1, source_target_pairs={{0,2},{1,5},{2,0},{3,7},{4,6},{5,1},{6,4},{7,3},{8,10},{9,13},{10,... | collective-permute-start | bytes 3145736 | tf_op jit(solution)/shard_map/ppermute | solution.py:33
  18.9 18.7 %collective-permute-start.2 = (f32[8,256]{1,0:T(8,128)S(1)}, f32[8,256]{1,0:T(8,128)S(1)}, u32[]{:S(2)}, u32[]{:S(2)}) collective-permute-start(f32[8,256]{1,0:T(8,128)S(1)} %bitcast.83), channel_id=1, source_target_pairs={{0,2},{1,5},{2,0},{3,7},{4,6},{5,1},{6,4},{7,3},{8,10},{9,13},{10,... | collective-permute-start | bytes 24584 | tf_op jit(solution)/shard_map/ppermute | solution.py:33
  20.9 28.0 %collective-permute-start.1 = (bf16[256,2048]{1,0:T(8,128)(2,1)}, bf16[256,2048]{1,0:T(8,128)(2,1)}, u32[]{:S(2)}, u32[]{:S(2)}) collective-permute-start(bf16[256,2048]{1,0:T(8,128)(2,1)} %param.21), channel_id=1, source_target_pairs={{0,2},{1,5},{2,0},{3,7},{4,6},{5,1},{6,4},{7,3},{8,10},{9,13},{10,... | collective-permute-start | bytes 3145736 | tf_op jit(solution)/shard_map/ppermute | solution.py:33
  26.2 13.2 %collective-permute-start.6 = (bf16[1,144,512]{2,1,0:T(8,128)(2,1)S(1)}, bf16[1,144,512]{2,1,0:T(8,128)(2,1)S(1)}, u32[]{:S(2)}, u32[]{:S(2)}) collective-permute-start(bf16[1,144,512]{2,1,0:T(8,128)(2,1)S(1)} %constant_dynamic-slice_fusion.15), channel_id=1, source_target_pairs={{0,4},{1,5},{2,6},{3,7},{4,0},{5,1},{6,2},{7,3},{8,12},{9,13},{10,... | collective-permute-start | bytes 442376 | tf_op jit(solution)/shard_map/ppermute | solution.py:33
  37.6 14.2 %collective-permute-start.3 = (f32[8,512]{1,0:T(8,128)S(1)}, f32[8,512]{1,0:T(8,128)S(1)}, u32[]{:S(2)}, u32[]{:S(2)}) collective-permute-start(f32[8,512]{1,0:T(8,128)S(1)} %pad_maximum_fusion.6), channel_id=1, source_target_pairs={{0,4},{1,3},{2,6},{3,1},{4,0},{5,7},{6,2},{7,5},{8,12},{9,11},{10,... | collective-permute-start | bytes 49160 | tf_op jit(solution)/shard_map/ppermute | solution.py:33
  39.4 9.5 %copy-start.23 = (bf16[256,2048]{1,0:T(8,128)(2,1)S(1)}, bf16[256,2048]{1,0:T(8,128)(2,1)}, u32[]{:S(2)}) copy-start(bf16[256,2048]{1,0:T(8,128)(2,1)} %param.21) | copy-start | bytes 3145732
  40.9 11.8 %copy-start = (bf16[512,2048]{1,0:T(8,128)(2,1)}, bf16[512,2048]{1,0:T(8,128)(2,1)S(1)}, u32[]{:S(2)}) copy-start(bf16[512,2048]{1,0:T(8,128)(2,1)S(1)} %pad_maximum_fusion.1.a_ref.xa_ref) | copy-start | bytes 6291460
  51.8 3.7 %collective-permute-start.10 = (f32[8,1024]{1,0:T(8,128)S(1)}, f32[8,1024]{1,0:T(8,128)S(1)}, u32[]{:S(2)}, u32[]{:S(2)}) collective-permute-start(f32[8,1024]{1,0:T(8,128)S(1)} %constant_dynamic-update-slice_fusion), channel_id=1, source_target_pairs={{0,1},{1,0},{2,3},{3,2},{4,5},{5,4},{6,7},{7,6},{8,9},{9,8},{10,11... | collective-permute-start | bytes 98312 | tf_op jit(solution)/shard_map/ppermute | solution.py:33
  52.6 37.8 %collective-permute-start.9 = (bf16[512,2048]{1,0:T(8,128)(2,1)S(1)}, bf16[512,2048]{1,0:T(8,128)(2,1)}, u32[]{:S(2)}, u32[]{:S(2)}) collective-permute-start(bf16[512,2048]{1,0:T(8,128)(2,1)S(1)} %pad_maximum_fusion.1.a_ref.xa_ref), channel_id=1, source_target_pairs={{0,1},{1,0},{2,3},{3,2},{4,5},{5,4},{6,7},{7,6},{8,9},{9,8},{10,11... | collective-permute-start | bytes 6291464 | tf_op jit(solution)/shard_map/ppermute | solution.py:33
  52.8 66.4 %collective-permute-start.7 = (bf16[512,2048]{1,0:T(8,128)(2,1)S(1)}, bf16[512,2048]{1,0:T(8,128)(2,1)}, u32[]{:S(2)}, u32[]{:S(2)}) collective-permute-start(bf16[512,2048]{1,0:T(8,128)(2,1)S(1)} %pad_maximum_fusion.1.a_ref.xa_ref), channel_id=1, source_target_pairs={{0,4},{1,3},{2,6},{3,1},{4,0},{5,7},{6,2},{7,5},{8,12},{9,11},{10,... | collective-permute-start | bytes 6291464 | tf_op jit(solution)/shard_map/ppermute | solution.py:33
  54.3 50.1 %collective-permute-start.13 = (bf16[512,2048]{1,0:T(8,128)(2,1)}, bf16[512,2048]{1,0:T(8,128)(2,1)}, u32[]{:S(2)}, u32[]{:S(2)}) collective-permute-start(bf16[512,2048]{1,0:T(8,128)(2,1)} %pad_maximum_fusion.2.a_ref.ca_ref), channel_id=1, source_target_pairs={{0,1},{1,0},{2,3},{3,2},{4,5},{5,4},{6,7},{7,6},{8,9},{9,8},{10,11... | collective-permute-start | bytes 6291464 | tf_op jit(solution)/shard_map/ppermute | solution.py:33
  54.3 64.8 %collective-permute-start.8 = (bf16[512,2048]{1,0:T(8,128)(2,1)}, bf16[512,2048]{1,0:T(8,128)(2,1)}, u32[]{:S(2)}, u32[]{:S(2)}) collective-permute-start(bf16[512,2048]{1,0:T(8,128)(2,1)} %pad_maximum_fusion.2.a_ref.ca_ref), channel_id=1, source_target_pairs={{0,4},{1,3},{2,6},{3,1},{4,0},{5,7},{6,2},{7,5},{8,12},{9,11},{10,... | collective-permute-start | bytes 6291464 | tf_op jit(solution)/shard_map/ppermute | solution.py:33
  55.5 6.2 %collective-permute-start.11 = (bf16[1,144,512]{2,1,0:T(8,128)(2,1)S(1)}, bf16[1,144,512]{2,1,0:T(8,128)(2,1)S(1)}, u32[]{:S(2)}, u32[]{:S(2)}) collective-permute-start(bf16[1,144,512]{2,1,0:T(8,128)(2,1)S(1)} %bitcast.75), channel_id=1, source_target_pairs={{0,8},{8,0},{16,24},{24,16},{1,9},{9,1},{17,25},{25,17},{2,10},{10... | collective-permute-start | bytes 442376 | tf_op jit(solution)/shard_map/ppermute | solution.py:78
  62.4 16.2 %collective-permute-start.12 = (bf16[2,144,512]{2,1,0:T(8,128)(2,1)}, bf16[2,144,512]{2,1,0:T(8,128)(2,1)}, u32[]{:S(2)}, u32[]{:S(2)}) collective-permute-start(bf16[2,144,512]{2,1,0:T(8,128)(2,1)} %pad_maximum_fusion.5), channel_id=1, source_target_pairs={{0,16},{8,24},{16,0},{24,8},{1,17},{9,25},{17,1},{25,9},{2,18},{10... | collective-permute-start | bytes 884744 | tf_op jit(solution)/shard_map/ppermute | solution.py:78
  104.4 15.3 %copy-start.1 = (bf16[512,2048]{1,0:T(8,128)(2,1)S(1)}, bf16[512,2048]{1,0:T(8,128)(2,1)}, u32[]{:S(2)}) copy-start(bf16[512,2048]{1,0:T(8,128)(2,1)} %copy-done) | copy-start | bytes 6291460
  119.1 10.5 %copy-start.14 = (f32[1024,2]{1,0:T(8,128)}, f32[1024,2]{1,0:T(8,128)S(1)}, u32[]{:S(2)}) copy-start(f32[1024,2]{1,0:T(8,128)S(1)} %get-tuple-element.164) | copy-start | bytes 24580
  119.1 10.5 %collective-permute-start.14 = (bf16[512,2048]{1,0:T(8,128)(2,1)}, bf16[512,2048]{1,0:T(8,128)(2,1)S(1)}, u32[]{:S(2)}, u32[]{:S(2)}) collective-permute-start(bf16[512,2048]{1,0:T(8,128)(2,1)} %collective-permute-done.7.a_ref.xa_ref), channel_id=1, source_target_pairs={{0,1},{1,0},{2,3},{3,2},{4,5},{5,4},{6,7},{7,6},{8,9},{9,8},{10,11... | collective-permute-start | bytes 6291464 | tf_op jit(solution)/shard_map/ppermute | solution.py:33
  119.2 10.4 %collective-permute-start.15 = (bf16[512,2048]{1,0:T(8,128)(2,1)}, bf16[512,2048]{1,0:T(8,128)(2,1)S(1)}, u32[]{:S(2)}, u32[]{:S(2)}) collective-permute-start(bf16[512,2048]{1,0:T(8,128)(2,1)} %collective-permute-done.8.a_ref.ca_ref), channel_id=1, source_target_pairs={{0,1},{1,0},{2,3},{3,2},{4,5},{5,4},{6,7},{7,6},{8,9},{9,8},{10,11... | collective-permute-start | bytes 6291464 | tf_op jit(solution)/shard_map/ppermute | solution.py:33
  129.6 13.9 %copy-start.18 = (bf16[512,2048]{1,0:T(8,128)(2,1)}, bf16[512,2048]{1,0:T(8,128)(2,1)S(1)}, u32[]{:S(2)}) copy-start(bf16[512,2048]{1,0:T(8,128)(2,1)S(1)} %collective-permute-done.15.b_ref.cb_ref) | copy-start | bytes 6291460
  129.6 46.8 %collective-permute-start.17 = (bf16[512,2048]{1,0:T(8,128)(2,1)}, bf16[512,2048]{1,0:T(8,128)(2,1)}, u32[]{:S(2)}, u32[]{:S(2)}) collective-permute-start(bf16[512,2048]{1,0:T(8,128)(2,1)} %get-tuple-element.143), channel_id=1, source_target_pairs={{0,1},{1,0},{2,3},{3,2},{4,5},{5,4},{6,7},{7,6},{8,9},{9,8},{10,11... | collective-permute-start | bytes 6291464 | tf_op jit(solution)/shard_map/ppermute | solution.py:33
  144.9 31.5 %collective-permute-start.16 = (bf16[512,2048]{1,0:T(8,128)(2,1)}, bf16[512,2048]{1,0:T(8,128)(2,1)}, u32[]{:S(2)}, u32[]{:S(2)}) collective-permute-start(bf16[512,2048]{1,0:T(8,128)(2,1)} %get-tuple-element.137), channel_id=1, source_target_pairs={{0,1},{1,0},{2,3},{3,2},{4,5},{5,4},{6,7},{7,6},{8,9},{9,8},{10,11... | collective-permute-start | bytes 6291464 | tf_op jit(solution)/shard_map/ppermute | solution.py:33
  159.7 12.5 %copy-start.15 = (f32[1024,2]{1,0:T(8,128)}, f32[1024,2]{1,0:T(8,128)S(1)}, u32[]{:S(2)}) copy-start(f32[1024,2]{1,0:T(8,128)S(1)} %get-tuple-element.165) | copy-start | bytes 24580
  179.0 29.0 %collective-permute-start.19 = (bf16[512,2048]{1,0:T(8,128)(2,1)S(1)}, bf16[512,2048]{1,0:T(8,128)(2,1)}, u32[]{:S(2)}, u32[]{:S(2)}) collective-permute-start(bf16[512,2048]{1,0:T(8,128)(2,1)S(1)} %shard_map.196), channel_id=1, source_target_pairs={{0,4},{1,3},{2,6},{3,1},{4,0},{5,7},{6,2},{7,5},{8,12},{9,11},{10,... | collective-permute-start | bytes 6291464 | tf_op jit(solution)/shard_map/ppermute | solution.py:33
  179.2 28.8 %collective-permute-start.18 = (bf16[512,2048]{1,0:T(8,128)(2,1)}, bf16[512,2048]{1,0:T(8,128)(2,1)}, u32[]{:S(2)}, u32[]{:S(2)}) collective-permute-start(bf16[512,2048]{1,0:T(8,128)(2,1)} %get-tuple-element.145), channel_id=1, source_target_pairs={{0,1},{1,0},{2,3},{3,2},{4,5},{5,4},{6,7},{7,6},{8,9},{9,8},{10,11... | collective-permute-start | bytes 6291464 | tf_op jit(solution)/shard_map/ppermute | solution.py:33
  179.5 28.5 %collective-permute-start.20 = (bf16[1152,512]{1,0:T(8,128)(2,1)}, bf16[1152,512]{1,0:T(8,128)(2,1)}, u32[]{:S(2)}, u32[]{:S(2)}) collective-permute-start(bf16[1152,512]{1,0:T(8,128)(2,1)} %get-tuple-element.148), channel_id=1, source_target_pairs={{0,8},{1,9},{2,10},{3,11},{4,12},{5,13},{6,14},{7,15}} | collective-permute-start | bytes 3538952 | tf_op jit(solution)/shard_map/ppermute | solution.py:69
  183.1 24.9 %collective-permute-start.21 = (bf16[1152,512]{1,0:T(8,128)(2,1)}, bf16[1152,512]{1,0:T(8,128)(2,1)}, u32[]{:S(2)}, u32[]{:S(2)}) collective-permute-start(bf16[1152,512]{1,0:T(8,128)(2,1)} %get-tuple-element.149), channel_id=1, source_target_pairs={{24,16},{25,17},{26,18},{27,19},{28,20},{29,21},{30,22},{31,23}} | collective-permute-start | bytes 3538952 | tf_op jit(solution)/shard_map/ppermute | solution.py:70
  184.8 27.6 %copy-start.7 = (bf16[512,2048]{1,0:T(8,128)(2,1)S(1)}, bf16[512,2048]{1,0:T(8,128)(2,1)}, u32[]{:S(2)}) copy-start(bf16[512,2048]{1,0:T(8,128)(2,1)} %copy-done.6) | copy-start | bytes 6291460
  212.4 15.2 %copy-start.5 = (bf16[512,2048]{1,0:T(8,128)(2,1)S(1)}, bf16[512,2048]{1,0:T(8,128)(2,1)}, u32[]{:S(2)}) copy-start(bf16[512,2048]{1,0:T(8,128)(2,1)} %copy-done.4) | copy-start | bytes 6291460
  216.5 44.0 %collective-permute-start.23 = (bf16[512,2048]{1,0:T(8,128)(2,1)}, bf16[512,2048]{1,0:T(8,128)(2,1)}, u32[]{:S(2)}, u32[]{:S(2)}) collective-permute-start(bf16[512,2048]{1,0:T(8,128)(2,1)} %shard_map.199), channel_id=1, source_target_pairs={{0,4},{1,3},{2,6},{3,1},{4,0},{5,7},{6,2},{7,5},{8,12},{9,11},{10,... | collective-permute-start | bytes 6291464 | tf_op jit(solution)/shard_map/ppermute | solution.py:33
  218.4 46.7 %collective-permute-start.26 = (bf16[512,2048]{1,0:T(8,128)(2,1)}, bf16[512,2048]{1,0:T(8,128)(2,1)}, u32[]{:S(2)}, u32[]{:S(2)}) collective-permute-start(bf16[512,2048]{1,0:T(8,128)(2,1)} %get-tuple-element.173), channel_id=1, source_target_pairs={{0,1},{1,0},{2,3},{3,2},{4,5},{5,4},{6,7},{7,6},{8,9},{9,8},{10,11... | collective-permute-start | bytes 6291464 | tf_op jit(solution)/shard_map/ppermute | solution.py:33
  220.4 12.4 %copy-start.28 = (s32[8]{0:T(128)S(1)}, s32[8]{0:T(128)}, u32[]{:S(2)}) copy-start(s32[8]{0:T(128)} %constant.136.clone) | copy-start | bytes 100
  220.4 15.6 %copy-start.27 = (s32[8]{0:T(128)S(1)}, s32[8]{0:T(128)}, u32[]{:S(2)}) copy-start(s32[8]{0:T(128)} %constant.135.clone) | copy-start | bytes 100
  220.4 73.0 %all-gather.5.cloned.1.call-start = ((), (), s32[]{:S(2)}) async-start(), calls=%async_computation.2 | async-start | bytes 1327104 | tf_op jit(solution)/shard_map/all_gather | solution.py:502
  220.4 40.1 %collective-permute-start.24 = (bf16[1152,512]{1,0:T(8,128)(2,1)}, bf16[1152,512]{1,0:T(8,128)(2,1)}, u32[]{:S(2)}, u32[]{:S(2)}) collective-permute-start(bf16[1152,512]{1,0:T(8,128)(2,1)} %get-tuple-element.167), channel_id=1, source_target_pairs={{0,8},{8,16},{1,9},{9,17},{2,10},{10,18},{3,11},{11,19},{4,12},{12... | collective-permute-start | bytes 3538952 | tf_op jit(solution)/shard_map/ppermute | solution.py:69
  225.9 34.6 %collective-permute-start.25 = (bf16[1152,512]{1,0:T(8,128)(2,1)}, bf16[1152,512]{1,0:T(8,128)(2,1)}, u32[]{:S(2)}, u32[]{:S(2)}) collective-permute-start(bf16[1152,512]{1,0:T(8,128)(2,1)} %get-tuple-element.168), channel_id=1, source_target_pairs={{24,16},{16,8},{25,17},{17,9},{26,18},{18,10},{27,19},{19,11},{28,... | collective-permute-start | bytes 3538952 | tf_op jit(solution)/shard_map/ppermute | solution.py:70
  232.5 25.8 %copy-start.11 = (bf16[256,2048]{1,0:T(8,128)(2,1)S(1)}, bf16[256,2048]{1,0:T(8,128)(2,1)}, u32[]{:S(2)}) copy-start(bf16[256,2048]{1,0:T(8,128)(2,1)} %copy-done.10) | copy-start | bytes 3145732
  232.5 25.8 %collective-permute-start.22 = (bf16[256,2048]{1,0:T(8,128)(2,1)}, bf16[256,2048]{1,0:T(8,128)(2,1)S(1)}, u32[]{:S(2)}, u32[]{:S(2)}) collective-permute-start(bf16[256,2048]{1,0:T(8,128)(2,1)} %get-tuple-element.161), channel_id=1, source_target_pairs={{0,2},{1,5},{2,0},{3,7},{4,6},{5,1},{6,4},{7,3},{8,10},{9,13},{10,... | collective-permute-start | bytes 3145736 | tf_op jit(solution)/shard_map/ppermute | solution.py:33
  260.5 4.6 %copy-start.3 = (bf16[512,2048]{1,0:T(8,128)(2,1)S(1)}, bf16[512,2048]{1,0:T(8,128)(2,1)}, u32[]{:S(2)}) copy-start(bf16[512,2048]{1,0:T(8,128)(2,1)} %copy-done.2) | copy-start | bytes 6291460
  265.1 15.7 %copy-start.24 = (f32[8,2,2048]{2,1,0:T(2,128)S(1)}, f32[8,2,2048]{2,1,0:T(2,128)}, u32[]{:S(2)}) copy-start(f32[8,2,2048]{2,1,0:T(2,128)} %all-gather.2) | copy-start | bytes 393220
  270.2 19.9 %collective-permute-start.27 = (bf16[256,2048]{1,0:T(8,128)(2,1)}, bf16[256,2048]{1,0:T(8,128)(2,1)}, u32[]{:S(2)}, u32[]{:S(2)}) collective-permute-start(bf16[256,2048]{1,0:T(8,128)(2,1)} %get-tuple-element.179), channel_id=1, source_target_pairs={{0,2},{1,5},{2,0},{3,7},{4,6},{5,1},{6,4},{7,3},{8,10},{9,13},{10,... | collective-permute-start | bytes 3145736 | tf_op jit(solution)/shard_map/ppermute | solution.py:33
  270.4 34.5 %collective-permute-start.28 = (bf16[1152,512]{1,0:T(8,128)(2,1)}, bf16[1152,512]{1,0:T(8,128)(2,1)S(1)}, u32[]{:S(2)}, u32[]{:S(2)}) collective-permute-start(bf16[1152,512]{1,0:T(8,128)(2,1)} %get-tuple-element.181), channel_id=1, source_target_pairs={{0,8},{8,16},{16,24},{1,9},{9,17},{17,25},{2,10},{10,18},{18,26},{... | collective-permute-start | bytes 3538952 | tf_op jit(solution)/shard_map/ppermute | solution.py:69
  279.5 29.4 %collective-permute-start.29 = (bf16[1152,512]{1,0:T(8,128)(2,1)}, bf16[1152,512]{1,0:T(8,128)(2,1)S(1)}, u32[]{:S(2)}, u32[]{:S(2)}) collective-permute-start(bf16[1152,512]{1,0:T(8,128)(2,1)} %get-tuple-element.182), channel_id=1, source_target_pairs={{24,16},{16,8},{8,0},{25,17},{17,9},{9,1},{26,18},{18,10},{10,2},{... | collective-permute-start | bytes 3538952 | tf_op jit(solution)/shard_map/ppermute | solution.py:70
  (13 other events, 24.9 us)
Sparse Core Ops, SparseCore 0:
  220.5 30.4 reduce-scatter.1
  260.7 29.8 all-gather.4

commit v2 on v1

--- a/solution.py
+++ b/solution.py
@@ -110,7 +110,7 @@
         out_shape=out_shape,
         cost_estimate=pl.CostEstimate(flops=1000, bytes_accessed=1000, transcendentals=0),
         compiler_params=pltpu.CompilerParams(
-            dimension_semantics=("arbitrary",), vmem_limit_bytes=48 * 1024 * 1024
+            dimension_semantics=("arbitrary",), vmem_limit_bytes=60 * 1024 * 1024
         ),
     )
 
@@ -315,70 +315,122 @@
     )(*arrays)
 
 
-def halves_of_sum(*arrays):
+def halves_of_sum(*arrays, split=()):
     half, width = arrays[0].shape[0] // 2, arrays[0].shape[1]
     tile = min(half, 128)
     tiles = half // tile
+    count = len(arrays)
 
     def body(*refs):
-        def run(out_ref):
+        def run(out_ref, more):
             total = refs[0][...].astype(F32)
-            for ref in refs[1:-2]:
+            for ref in refs[1:count] + more:
                 total = total + ref[...].astype(F32)
             out_ref[...] = total.astype(BF)
 
-        on_both(tiles, run, (refs[-2],), (refs[-1],))
+        more = refs[count:-2]
+        on_both(tiles, run, (refs[-2], more[:1]), (refs[-1], more[1:]))
 
     shape = jax.ShapeDtypeStruct((half, width), BF)
+    ends = [first_rows(tile, width, tiles), second_rows(tile, width, tiles)]
     return call(
         body,
         (2 * tiles,),
-        [by_rows(tile, width)] * len(arrays),
-        [first_rows(tile, width, tiles), second_rows(tile, width, tiles)],
+        [by_rows(tile, width)] * count + ends[: len(split)],
+        ends,
         [shape, shape],
-    )(*arrays)
-
-
-def fold(*arrays):
+    )(*arrays, *split)
+
+
+def last_hop(mine, other):
+    step = len(chip_bits()) - 1
+    return [hop(part, step) for part in halves_of_sum(mine, other)]
+
+
+def fold(mine, got):
+    arrays, split = ((mine,), tuple(got)) if isinstance(got, list) else ((mine, got), ())
     for step in range(len(chip_bits()) - 2, -1, -1):
-        mine, other = halves_of_sum(*arrays)
-        arrays = (mine, hop(other, step))
+        mine, other = halves_of_sum(*arrays, split=split)
+        arrays, split = (mine, hop(other, step)), ()
     return sum_of(*arrays)
 
 
 def finish(mine, right, left, hot, is_owner):
     units, width = hot.shape[1:]
 
-    def body(flag_ref, mine_ref, right_ref, left_ref, hot_ref, out_ref):
-        total = mine_ref[...].astype(F32) + right_ref[...].astype(F32) + left_ref[...].astype(F32)
-        total = jnp.where(flag_ref[0] > 0, hot_ref[0].astype(F32), total)
-        out_ref[0] = total.T
-
-    block = pl.BlockSpec((units, width), lambda i: (i, 0))
+    def body(flag_ref, mine_ref, right_ref, left_ref, hot_ref, *out_refs):
+        for index, out_ref in enumerate(out_refs):
+            rows = slice(index * units, (index + 1) * units)
+            total = mine_ref[rows].astype(F32) + right_ref[rows].astype(F32) + left_ref[rows].astype(F32)
+            total = jnp.where(flag_ref[0] > 0, hot_ref[index].astype(F32), total)
+            out_ref[0] = total.T
+
+    block = whole((3 * units, width))
     return pl.pallas_call(
         body,
-        grid=(3,),
+        grid=(1,),
         in_specs=[
             pl.BlockSpec(memory_space=pltpu.SMEM), block, block, block,
-            pl.BlockSpec((1, units, width), lambda i: (i, 0, 0)),
-        ],
-        out_specs=pl.BlockSpec((1, width, units), lambda i: (i, 0, 0)),
-        out_shape=jax.ShapeDtypeStruct((3, width, units), F32),
-        compiler_params=pltpu.CompilerParams(vmem_limit_bytes=32 * 1024 * 1024),
+            pl.BlockSpec((3, units, width), lambda i: (0, 0, 0)),
+        ],
+        out_specs=[pl.BlockSpec((1, width, units), lambda i: (0, 0, 0))] * 3,
+        out_shape=[jax.ShapeDtypeStruct((1, width, units), F32)] * 3,
+        compiler_params=pltpu.CompilerParams(vmem_limit_bytes=60 * 1024 * 1024),
     )(is_owner.astype(jnp.int32).reshape(1), mine, right, left, hot)
 
 
 def hot_pieces(weights, is_owner):
-    experts, groups = lax.axis_size("expert"), lax.axis_size("dp")
     width, units = weights[0].shape
-    part = width // groups
-    start = lax.axis_index("dp") * part
-    pieces = [
-        lax.dynamic_slice_in_dim(w, start, part, 0).T.reshape(experts, units // experts, part)
-        for w in weights
-    ]
-    pieces = jnp.concatenate(pieces, axis=1)
-    return jnp.where(is_owner, pieces, jnp.zeros_like(pieces))
+    part = width // lax.axis_size("dp")
+    scalars = jnp.stack([lax.axis_index("dp"), is_owner.astype(jnp.int32)]).astype(jnp.int32)
+
+    def body(scalar_ref, a_ref, b_ref, c_ref, out_ref):
+        for index, ref in enumerate((a_ref, b_ref, c_ref)):
+            out_ref[index] = ref[...].T
+
+        @pl.when(scalar_ref[1] == 0)
+        def _():
+            out_ref[...] = jnp.zeros_like(out_ref)
+
+    return pl.pallas_call(
+        body,
+        grid_spec=pltpu.PrefetchScalarGridSpec(
+            num_scalar_prefetch=1,
+            grid=(1,),
+            in_specs=[pl.BlockSpec((part, units), lambda i, scalars: (scalars[0], 0))] * 3,
+            out_specs=pl.BlockSpec((3, units, part), lambda i, scalars: (0, 0, 0)),
+        ),
+        out_shape=jax.ShapeDtypeStruct((3, units, part), BF),
+        cost_estimate=pl.CostEstimate(flops=1000, bytes_accessed=1000, transcendentals=0),
+        compiler_params=pltpu.CompilerParams(vmem_limit_bytes=60 * 1024 * 1024),
+    )(scalars, *weights)
+
+
+def widen(weights, hot):
+    width, units = weights[0].shape
+    spare = hot.shape[1]
+    tile = tile_of(width)
+
+    def body(gate_ref, up_ref, down_ref, hot_ref, in_ref, out_ref):
+        padded = units + spare
+        in_ref[:, :units] = gate_ref[...]
+        in_ref[:, units:padded] = hot_ref[0].T
+        in_ref[:, padded : padded + units] = up_ref[...]
+        in_ref[:, padded + units :] = hot_ref[1].T
+        out_ref[:, :units] = down_ref[...]
+        out_ref[:, units:] = hot_ref[2].T
+
+    rows = by_rows(tile, units)
+    return call(
+        body,
+        (width // tile,),
+        [rows, rows, rows, pl.BlockSpec((3, spare, tile), lambda i: (0, 0, i))],
+        [by_rows(tile, 2 * (units + spare)), by_rows(tile, units + spare)],
+        [
+            jax.ShapeDtypeStruct((width, 2 * (units + spare)), BF),
+            jax.ShapeDtypeStruct((width, units + spare), BF),
+        ],
+    )(*weights, hot)
 
 
 def per_device(tokens, expert_ids, gates, w_gate, w_up, w_down, cotangent):
@@ -391,28 +443,34 @@
     expert_range = jnp.arange(experts, dtype=jnp.int32)
     matches = expert_ids[:, :, None] == expert_range
     hot_expert = jnp.argmax(jnp.sum(matches.astype(jnp.int32), axis=(0, 1))).astype(jnp.int32)
-    is_owner = me == hot_expert
+    is_owner = jnp.sum((expert_ids == me).astype(jnp.int32)) == tok_rows
     is_me = ((expert_range == me) & ~is_owner)[:, None]
     is_hot = (expert_range == hot_expert)[:, None]
     routed = jnp.sum(jnp.where(matches, gates[:, :, None], 0.0), axis=1).T
     own = (w_gate[0], w_up[0], w_down[0])
     orders = row_order()
-    x_held, c_held, r_held = tokens, cotangent, routed
-    for step in range(last):
+    def halve(value, bit):
+        value = value.reshape(3, value.shape[1] // 2, 2, share, width // groups)
+        mark = (me // bit) % 2
+        other = lax.dynamic_index_in_dim(value, 1 - mark, 2, keepdims=False)
+        return lax.dynamic_index_in_dim(value, mark, 2, keepdims=False) + flip(other, bit, bit)
+
+    x_got, c_got, r_got = hop(tokens, 0), hop(cotangent, 0), hop(routed, 0)
+    hot = hot_pieces(own, is_owner).reshape(3, experts, share, width // groups)
+    hot = halve(hot, 1)
+    x_got, c_got, r_got, hot = ends_round(x_got, c_got, r_got, hot)
+
+    x_held, c_held = join(tokens, x_got), join(cotangent, c_got)
+    r_held = jnp.concatenate([routed, r_got], axis=1)
+    for step in range(1, last):
         x_held = join(x_held, hop(x_held, step))
         c_held = join(c_held, hop(c_held, step))
         r_held = jnp.concatenate([r_held, hop(r_held, step)], axis=1)
+    bit = 2
+    while bit < experts:
+        hot = halve(hot, bit)
+        bit *= 2
     r_last = hop(r_held, last)
-    hot = hot_pieces(own, is_owner)
-    bit = 1
-    while bit < experts:
-        hot = hot.reshape((hot.shape[0] // 2, 2) + hot.shape[1:])
-        mark = (me // bit) % 2
-        other = lax.dynamic_index_in_dim(hot, 1 - mark, 1, keepdims=False)
-        hot = lax.dynamic_index_in_dim(hot, mark, 1, keepdims=False)
-        hot = hot + flip(other, bit, bit)
-        bit *= 2
-    hot = hot[0]
     x_held, c_held, r_held, r_last, hot = ends_round(x_held, c_held, r_held, r_last, hot)
 
     x_last, c_last = hop(x_held, last), hop(c_held, last)
@@ -432,11 +490,9 @@
         return jnp.stack(columns).T
 
     gate_near, gate_far = gates_of(slice(None, half)), gates_of(slice(half, None))
+    hot = line_gather(hot.reshape(3 * share, width // groups)).reshape(3, share, width)
     spare = share + -(units + share) % 128
-    hot = line_gather(hot).reshape(3, share, width)
-    hot = jnp.pad(hot, ((0, 0), (0, spare - share), (0, 0))).reshape(3 * spare, width).T
-    w_in = jnp.concatenate([own[0], hot[:, :spare], own[1], hot[:, spare : 2 * spare]], axis=1)
-    w_out = jnp.concatenate([own[2], hot[:, 2 * spare :]], axis=1)
+    w_in, w_out = widen(own, jnp.pad(hot, ((0, 0), (0, spare - share), (0, 0))))
     a_near, s_near, m_near, m_near_far = forward(x_held, x_other, gate_near, w_in, w_out, units)
     p_near, t_near, t_near_far, d_near = backward(
         c_held, c_other, a_near, gate_near, w_in, w_out, units
@@ -464,31 +520,35 @@
     p_far, t_far, t_far_far, d_far = backward(
         c_last, c_last_other, a_far, gate_far, w_in, w_out, units
     )
+    t_far_other = swap_core(t_far_far)
     own_grad, hot_grad = weight_totals(
         p_far, (x_last, x_last_other), s_far, (c_last, c_last_other), in_near, down_near, units
     )
     line = LineSum(own_grad)
     right, left = line.sends(1)
-    right, left, m_far, m_far_other, t_far, t_far_far, d_far, hot_grad, m_near, m_near_other = ends_round(
-        right, left, m_far, m_far_other, t_far, t_far_far, d_far, hot_grad, m_near, m_near_other
+    (
+        right, left, m_far, m_far_other, t_far, t_far_other, d_far, hot_grad,
+        m_near, m_near_other, t_near, t_near_other,
+    ) = ends_round(
+        right, left, m_far, m_far_other, t_far, t_far_other, d_far, hot_grad,
+        m_near, m_near_other, t_near, t_near_other,
     )
 
     line.send(1, right, left)
-    m_got = hop(sum_of(m_far, m_far_other), last)
-    t_far_other = swap_core(t_far_far)
+    m_got = last_hop(m_far, m_far_other)
+    t_far = sum_of(t_far, t_far_other)
+    m_near, t_near = sum_of(m_near, m_near_other), sum_of(t_near, t_near_other)
     hot_grad = hot_grad.reshape(3, spare, width)[:, :share].reshape(3 * share, width)
     hot_sum = lax.psum_scatter(hot_grad, "dp", scatter_dimension=1, tiled=True)
-    t_far, t_far_other, m_got, line.right, line.left = ends_round(
-        t_far, t_far_other, m_got, line.right, line.left
+    t_far, m_near, t_near, line.right, line.left, *m_got = ends_round(
+        t_far, m_near, t_near, line.right, line.left, *m_got
     )
 
     right, left = line.sends(2)
-    right, left, t_far, t_far_other, m_got, m_near, m_near_other = ends_round(
-        right, left, t_far, t_far_other, m_got, m_near, m_near_other
-    )
+    right, left, t_far, m_near, *m_got = ends_round(right, left, t_far, m_near, *m_got)
     line.send(2, right, left)
-    t_got = hop(sum_of(t_far, t_far_other), last)
-    mixed = fold(m_near, m_near_other, m_got)
+    t_got = hop(t_far, last)
+    mixed = fold(m_near, m_got)
     dots = lax.all_gather(jnp.concatenate([d_near, d_far]).T, "expert", axis=0)
     mixed, t_got, dots, hot_sum, line.right, line.left = ends_round(
         mixed, t_got, dots, hot_sum, line.right, line.left
@@ -496,9 +556,9 @@
 
     for step in range(3, groups):
         right, left = line.sends(step)
-        right, left, t_near, t_near_other, t_got = ends_round(right, left, t_near, t_near_other, t_got)
+        right, left, t_near, t_got = ends_round(right, left, t_near, t_got)
         line.send(step, right, left)
-    tokens_grad = fold(t_near, t_near_other, t_got)
+    tokens_grad = fold(t_near, t_got)
     hot_all = lax.all_gather(hot_sum.astype(BF), "expert", axis=0)
 
     my_dots = []
@@ -515,7 +575,7 @@
     hot_all = hot_all.reshape(experts, 3, share, width // groups)
     hot_all = jnp.moveaxis(hot_all, 1, 0).reshape(3, units, width // groups)
     grads = finish(line.block(group), line.right, line.left, hot_all, is_owner)
-    return (mixed, tokens_grad, gates_grad, grads[0:1], grads[1:2], grads[2:3])
+    return (mixed, tokens_grad, gates_grad, *grads)
 
 
 def solution(mesh):

time: 319 us -> 310 us (0.972)
  Pallas kernels: 93 us -> 126 us
  waiting for transfers between devices: 80.9 us -> 62.6 us
  local copies, waits for them, and re-layouts: 35.6 us -> 20.9 us
  starting transfers between devices: 43.8 us -> 35.9 us
  other arithmetic: 27.9 us -> 21.4 us
  blocking collectives: 16.6 us -> 21.3 us
    ppermute x3, waiting for transfers between devices: 34.3 us -> 6.31 us  [send(): self.right = lax.ppermute(right, 'dp', [(i, i + 1) for i in range(step)])]
    pallas_call x3 -> x6, Pallas kernels: 8.87 us -> 29.3 us  [the longest x3 13.7 us: halves_of_sum(): call(body, (2 * tiles,), [by_rows(tile, width)] * count + ends[:len(split...]
    ppermute x3, starting transfers between devices: 18.2 us -> 7.16 us  [send(): self.right = lax.ppermute(right, 'dp', [(i, i + 1) for i in range(step)])]
    ppermute x22 -> x23, waiting for transfers between devices: 25 us -> 35.7 us  [flip(): return lax.ppermute(value, 'expert', pairs)]
    unnamed x59 -> x29, local copies, waits for them, and re-layouts: 11 us -> 1.85 us
    pallas_call x4 -> x5, Pallas kernels: 9.92 us -> 17.8 us  [sum_of(): call(body, (rows // tile,), [by_rows(tile, width)] * len(arrays), by_rows...]
    all_gather x1, blocking collectives: 16.6 us -> 21.3 us  [per_device(): dots = lax.all_gather(jnp.concatenate([d_near, d_far]).T, 'expert', axis=0)]
    concatenate x3 -> x1, other arithmetic: 3.81 us -> 0.01 us  [per_device(): r_held = jnp.concatenate([routed, r_got], axis=1)]
  transfers between devices with their start and end apart: 32 -> 33, of which waited for: 11 -> 10; matrix products, arithmetic and copies ran while one was open for 13% -> 12% of each run, Pallas kernels for 27% -> 40%
where the time goes in v2:
time: 310 us; the launch traced here: 308 us
  Pallas kernels  126 us (41%)
  waiting for transfers between devices  62.6 us (20%)
  starting transfers between devices  35.9 us (12%)
  other arithmetic  21.4 us (7%)
  blocking collectives  21.3 us (7%)
  local copies, waits for them, and re-layouts  20.9 us (7%)
  between operations  20.2 us (7%)
    ppermute x23, waiting for transfers between devices, flip(): return lax.ppermute(value, 'expert', pairs)  35.7 us
    pallas_call x2, Pallas kernels, backward(): call(body, (2 * tiles,), [first_rows(tile, width, tiles), second_rows(til...  27.4 us
    pallas_call x2, Pallas kernels, forward(): call(body, (2 * tiles,), [first_rows(tile, width, tiles), second_rows(til...  26.1 us
    all_gather x1, blocking collectives, per_device(): dots = lax.all_gather(jnp.concatenate([d_near, d_far]).T, 'expert', axis=0)  21.3 us
    ppermute x23, starting transfers between devices, flip(): return lax.ppermute(value, 'expert', pairs)  19.8 us
    pallas_call x5, Pallas kernels, sum_of(): call(body, (rows // tile,), [by_rows(tile, width)] * len(arrays), by_rows...  17.8 us
    ppermute x2, waiting for transfers between devices, line_gather(): lax.ppermute(found, 'dp', [(i, i ^ bit) for i in range(groups)])  16.7 us
    pallas_call x1, Pallas kernels, weight_totals(): call(body, (width // tile,), [whole(pre.shape), cut, cut, whole(hidden.sh...  14.1 us
  transfers between devices with their start and end apart: 33, of which 10 were waited for; matrix products, arithmetic and copies ran while one was open for 12% of the time, Pallas kernels for 40%

profile of v2, /device:TPU:0, one launch (start us, length us, event | category | flops | bytes accessed | tf_op | source)
XLA Modules:
  0.0 308.4 jit_solution(2531468793480138547)
XLA Ops:
  7.2 3.0 collective-permute-start
  12.9 3.5 %shard_map.190 = bf16[3,384,512]{2,1,0:T(8,128)(2,1)} custom-call(s32[2]{0:T(128)} %pad_add_fusion.scalar_ref, bf16[2048,384]{1,0:T(8,128)(2,1)} %bitcast.41, bf16[2048,384]{1,0:T(8,128)(2,1)} %bitcast.43, bf16[2048,384]{1,0:T(8,128)(2,1)} %bitcast.45), custom_call_target="tpu_custom_call" | custom-call | flops 1000 | bytes 1000 | tf_op jit(solution)/shard_map/pallas_call | solution.py:395
  16.4 1.9 dynamic-slice_bitcast_fusion
  18.3 1.9 collective-permute-start.2
  21.9 12.6 %collective-permute-done.2 = f32[8,256]{1,0:T(8,128)S(1)} collective-permute-done((f32[8,256]{1,0:T(8,128)S(1)}, f32[8,256]{1,0:T(8,128)S(1)}, u32[]{:S(2)}, u32[]{:S(2)}) %collective-permute-start.2) | collective-permute-done | bytes 8224 | tf_op jit(solution)/shard_map/ppermute | solution.py:33
  34.6 2.1 collective-permute-start.5
  37.3 1.5 collective-permute-start.4
  38.9 4.2 %collective-permute-done.5 = bf16[3,2,48,512]{3,2,1,0:T(8,128)(2,1)S(1)} collective-permute-done((bf16[3,2,48,512]{3,2,1,0:T(8,128)(2,1)S(1)}, bf16[3,2,48,512]{3,2,1,0:T(8,128)(2,1)S(1)}, u32[]{:S(2)}, u32[]{:S(2)}) %collective-permute-start.5) | collective-permute-done | bytes 294944 | tf_op jit(solution)/shard_map/ppermute | solution.py:33
  43.1 1.8 collective-permute-start.6
  44.9 3.6 %pad_maximum_fusion = (bf16[512,2048]{1,0:T(8,128)(2,1)S(1)}, bf16[512,2048]{1,0:T(8,128)(2,1)}) fusion(bf16[256,2048]{1,0:T(8,128)(2,1)} %copy-done.7, bf16[256,2048]{1,0:T(8,128)(2,1)S(1)} %copy-done.6, bf16[256,2048]{1,0:T(8,128)(2,1)} %copy-done.8, bf16[256,2048]{1,0:T(8,128)(2,1)} %param.21), kind=kLoop, calls=%fused_computation.9 | loop fusion | flops 8388608 | bytes 8388608 | tf_op jit(solution)/shard_map/concatenate | solution.py:19
  49.9 1.5 collective-permute-start.7
  52.7 1.6 collective-permute-start.11
  55.5 3.4 %collective-permute-done.11 = bf16[1,144,512]{2,1,0:T(8,128)(2,1)S(1)} collective-permute-done((bf16[1,144,512]{2,1,0:T(8,128)(2,1)S(1)}, bf16[1,144,512]{2,1,0:T(8,128)(2,1)S(1)}, u32[]{:S(2)}, u32[]{:S(2)}) %collective-permute-start.11) | collective-permute-done | bytes 147488 | tf_op jit(solution)/shard_map/ppermute | solution.py:78
  59.0 2.7 collective-permute-start.12
  61.6 13.3 %collective-permute-done.12 = bf16[2,144,512]{2,1,0:T(8,128)(2,1)S(1)} collective-permute-done((bf16[2,144,512]{2,1,0:T(8,128)(2,1)S(1)}, bf16[2,144,512]{2,1,0:T(8,128)(2,1)S(1)}, u32[]{:S(2)}, u32[]{:S(2)}) %collective-permute-start.12) | collective-permute-done | bytes 294944 | tf_op jit(solution)/shard_map/ppermute | solution.py:78
  77.4 8.1 %shard_map.191 = (bf16[2048,1024]{1,0:T(8,128)(2,1)}, bf16[2048,512]{1,0:T(8,128)(2,1)}) custom-call(bf16[2048,384]{1,0:T(8,128)(2,1)} %bitcast.42, bf16[2048,384]{1,0:T(8,128)(2,1)} %bitcast.44, bf16[2048,384]{1,0:T(8,128)(2,1)} %bitcast.46, bf16[3,128,2048]{2,1,0:T(8,128)(2,1)} %fusion.6.hot_ref), custom_call_target="tpu_custom_call" | custom-call | flops 1000 | bytes 1000 | tf_op jit(solution)/shard_map/pallas_call | solution.py:424
  85.5 13.0 %shard_map.192 = (f32[1024,1024]{1,0:T(8,128)}, bf16[512,1024]{1,0:T(8,128)(2,1)}, bf16[512,2048]{1,0:T(8,128)(2,1)}, bf16[512,2048]{1,0:T(8,128)(2,1)}) custom-call(bf16[512,2048]{1,0:T(8,128)(2,1)} %copy-done, bf16[512,2048]{1,0:T(8,128)(2,1)} %collective-permute-done.9.b_ref.xb_ref, f32[1024,2]{1,0:T(8,128)} %bitcast.52, ...), custom_call_target="tpu_custom_call" | custom-call | flops 1000 | bytes 1000 | tf_op jit(solution)/shard_map/pallas_call | solution.py:169
  98.5 13.7 %shard_map.193 = (bf16[1024,1024]{1,0:T(8,128)(2,1)}, bf16[512,2048]{1,0:T(8,128)(2,1)}, bf16[512,2048]{1,0:T(8,128)(2,1)}, f32[1024,2]{1,0:T(8,128)}) custom-call(bf16[512,2048]{1,0:T(8,128)(2,1)} %get-tuple-element.138.a_ref.ca_ref, bf16[512,2048]{1,0:T(8,128)(2,1)} %collective-permute-done.13.b_ref.cb_ref, f32[1024,1024]{1,0:T(8,128)} %get-tuple-element.122.act_ref, ...), custom_call_target="tpu_custom_call" | custom-call | flops 1000 | bytes 1000 | tf_op jit(solution)/shard_map/pallas_call | solution.py:220
  112.8 11.5 %shard_map.194 = (f32[1024,2048]{1,0:T(8,128)}, f32[512,2048]{1,0:T(8,128)}) custom-call(bf16[1024,1024]{1,0:T(8,128)(2,1)} %get-tuple-element.134.pre_ref, bf16[512,2048]{1,0:T(8,128)(2,1)} %copy-done, bf16[512,2048]{1,0:T(8,128)(2,1)} %collective-permute-done.9.b_ref.xb_ref, bf16[512,1024]{1,0:T(8,128)(2,1)} %get-tuple-element.137.hidden_ref, ...), custom_call_target="tpu_custom_call" | custom-call | flops 1000 | bytes 1000 | tf_op jit(solution)/shard_map/pallas_call | solution.py:249
  125.6 13.0 %shard_map.195 = (f32[1024,1024]{1,0:T(8,128)}, bf16[512,1024]{1,0:T(8,128)(2,1)}, bf16[512,2048]{1,0:T(8,128)(2,1)}, bf16[512,2048]{1,0:T(8,128)(2,1)}) custom-call(bf16[512,2048]{1,0:T(8,128)(2,1)} %collective-permute-done.7.a_ref.xa_ref, bf16[512,2048]{1,0:T(8,128)(2,1)} %copy-done.1, f32[1024,2]{1,0:T(8,128)} %bitcast.50, ...), custom_call_target="tpu_custom_call" | custom-call | flops 1000 | bytes 1000 | tf_op jit(solution)/shard_map/pallas_call | solution.py:169
  138.7 13.7 %shard_map.196 = (bf16[1024,1024]{1,0:T(8,128)(2,1)}, bf16[512,2048]{1,0:T(8,128)(2,1)}, bf16[512,2048]{1,0:T(8,128)(2,1)}, f32[1024,2]{1,0:T(8,128)}) custom-call(bf16[512,2048]{1,0:T(8,128)(2,1)} %collective-permute-done.8.a_ref.ca_ref, bf16[512,2048]{1,0:T(8,128)(2,1)} %collective-permute-done.15.b_ref.cb_ref, f32[1024,1024]{1,0:T(8,128)} %get-tuple-element.149.act_ref, ...), custom_call_target="tpu_custom_call" | custom-call | flops 1000 | bytes 1000 | tf_op jit(solution)/shard_map/pallas_call | solution.py:220
  152.9 14.1 %shard_map.197 = (bf16[1152,2048]{1,0:T(8,128)(2,1)}, bf16[384,2048]{1,0:T(8,128)(2,1)}) custom-call(bf16[1024,1024]{1,0:T(8,128)(2,1)} %get-tuple-element.150.pre_ref, bf16[512,2048]{1,0:T(8,128)(2,1)} %collective-permute-done.7.a_ref.xa_ref, bf16[512,2048]{1,0:T(8,128)(2,1)} %copy-done.1, bf16[512,1024]{1,0:T(8,128)(2,1)} %get-tuple-element.151.hidden_ref, ...), custom_call_target="tpu_custom_call" | custom-call | flops 1000 | bytes 1000 | tf_op jit(solution)/shard_map/pallas_call | solution.py:284
  167.0 3.8 %constant_dynamic-slice_fusion = (bf16[1152,512]{1,0:T(8,128)(2,1)}, bf16[1152,512]{1,0:T(8,128)(2,1)S(1)}, bf16[1152,512]{1,0:T(8,128)(2,1)}) fusion(bf16[1152,2048]{1,0:T(8,128)(2,1)} %get-tuple-element.154, s32[]{:T(128)S(6)} %select_n.200, s32[]{:T(128)S(6)} %select_n.178, s32[]{:T(128)S(6)} %select_n.177), kind=kLoop, calls=%fused_computation.35 | loop fusion | bytes 7077900 | tf_op jit(solution)/shard_map/dynamic_slice | solution.py:58
  170.9 3.5 %collective-permute-start.20 = (bf16[1152,512]{1,0:T(8,128)(2,1)}, bf16[1152,512]{1,0:T(8,128)(2,1)}, u32[]{:S(2)}, u32[]{:S(2)}) collective-permute-start(bf16[1152,512]{1,0:T(8,128)(2,1)} %get-tuple-element.171), channel_id=1, source_target_pairs={{0,8},{1,9},{2,10},{3,11},{4,12},{5,13},{6,14},{7,15}} | collective-permute-start | bytes 3538952 | tf_op jit(solution)/shard_map/ppermute | solution.py:69
  174.4 1.7 collective-permute-start.21
  176.0 4.5 %shard_map.201 = (bf16[256,2048]{1,0:T(8,128)(2,1)}, bf16[256,2048]{1,0:T(8,128)(2,1)}) custom-call(bf16[512,2048]{1,0:T(8,128)(2,1)} %get-tuple-element.173.refs_0_, bf16[512,2048]{1,0:T(8,128)(2,1)} %collective-permute-done.16.refs_1_), custom_call_target="tpu_custom_call" | custom-call | flops 1000 | bytes 1000 | tf_op jit(solution)/shard_map/pallas_call | solution.py:336
  180.7 1.8 collective-permute-start.23
  182.5 4.3 %shard_map.198 = bf16[512,2048]{1,0:T(8,128)(2,1)} custom-call(bf16[512,2048]{1,0:T(8,128)(2,1)} %get-tuple-element.165.refs_0_, bf16[512,2048]{1,0:T(8,128)(2,1)} %copy-done.3), custom_call_target="tpu_custom_call" | custom-call | flops 1000 | bytes 1000 | tf_op jit(solution)/shard_map/pallas_call | solution.py:309
  186.9 4.3 %shard_map.199.refs_0_ = bf16[512,2048]{1,0:T(8,128)(2,1)} custom-call(bf16[512,2048]{1,0:T(8,128)(2,1)} %get-tuple-element.167.refs_0_, bf16[512,2048]{1,0:T(8,128)(2,1)} %collective-permute-done.18.refs_1_), custom_call_target="tpu_custom_call" | custom-call | flops 1000 | bytes 1000 | tf_op jit(solution)/shard_map/pallas_call | solution.py:309
  191.2 4.3 %shard_map.200.refs_0_ = bf16[512,2048]{1,0:T(8,128)(2,1)} custom-call(bf16[512,2048]{1,0:T(8,128)(2,1)} %get-tuple-element.169.refs_0_, bf16[512,2048]{1,0:T(8,128)(2,1)} %collective-permute-done.19.refs_1_), custom_call_target="tpu_custom_call" | custom-call | flops 1000 | bytes 1000 | tf_op jit(solution)/shard_map/pallas_call | solution.py:309
  195.6 11.2 %collective-permute-done.23.refs_2_ = bf16[256,2048]{1,0:T(8,128)(2,1)} collective-permute-done((bf16[256,2048]{1,0:T(8,128)(2,1)}, bf16[256,2048]{1,0:T(8,128)(2,1)}, u32[]{:S(2)}, u32[]{:S(2)}) %collective-permute-start.23) | collective-permute-done | bytes 1048608 | tf_op jit(solution)/shard_map/ppermute | solution.py:33
  206.9 4.0 %add_convert_fusion.2 = (bf16[1152,512]{1,0:T(8,128)(2,1)S(1)}, bf16[1152,512]{1,0:T(8,128)(2,1)}) fusion(bf16[1152,512]{1,0:T(8,128)(2,1)} %collective-permute-done.21, bf16[1152,2048]{1,0:T(8,128)(2,1)} %get-tuple-element.154, s32[]{:T(128)S(6)} %select_n.179, bf16[1152,512]{1,0:T(8,128)(2,1)} %collective-permute-done.20, s32[]{:T(128)S(6)} %select_n.176), kind=kLoop, calls=%fused_computation.7 | loop fusion | flops 4718592 | bytes 7077896 | tf_op jit(solution)/shard_map/convert_element_type | solution.py:15
  211.1 1.9 slice.76
  213.1 2.3 collective-permute-start.26
  215.4 1.7 collective-permute-start.27
  217.1 4.6 %shard_map.202 = (bf16[256,2048]{1,0:T(8,128)(2,1)}, bf16[256,2048]{1,0:T(8,128)(2,1)}) custom-call(bf16[512,2048]{1,0:T(8,128)(2,1)} %shard_map.199.refs_0_, bf16[256,2048]{1,0:T(8,128)(2,1)} %collective-permute-done.22.refs_1_, bf16[256,2048]{1,0:T(8,128)(2,1)} %collective-permute-done.23.refs_2_), custom_call_target="tpu_custom_call" | custom-call | flops 1000 | bytes 1000 | tf_op jit(solution)/shard_map/pallas_call | solution.py:336
  230.8 21.3 %all-gather.2 = f32[8,2,2048]{2,1,0:T(2,128)} all-gather(f32[1,2,2048]{2,1,0:T(2,128)S(1)} %maximum_bitcast_fusion), channel_id=2, replica_groups=mesh['dp'=4,'expert'=8] {'expert'}, dimensions={0}, use_global_device_ids=true | all-gather | bytes 147456 | tf_op jit(solution)/shard_map/all_gather | solution.py:552
  252.2 2.4 shard_map.203
  254.6 4.0 %add_convert_fusion = (bf16[1152,512]{1,0:T(8,128)(2,1)S(1)}, bf16[1152,512]{1,0:T(8,128)(2,1)}) fusion(bf16[1152,512]{1,0:T(8,128)(2,1)} %collective-permute-done.27, bf16[1152,2048]{1,0:T(8,128)(2,1)} %get-tuple-element.154, s32[]{:T(128)S(6)} %select_n.181, bf16[1152,512]{1,0:T(8,128)(2,1)} %collective-permute-done.26, s32[]{:T(128)S(6)} %select_n.180), kind=kLoop, calls=%fused_computation.5 | loop fusion | flops 4718592 | bytes 7077896 | tf_op jit(solution)/shard_map/convert_element_type | solution.py:15
  258.7 4.6 %shard_map.204 = (bf16[256,2048]{1,0:T(8,128)(2,1)}, bf16[256,2048]{1,0:T(8,128)(2,1)}) custom-call(bf16[512,2048]{1,0:T(8,128)(2,1)} %shard_map.200.refs_0_, bf16[512,2048]{1,0:T(8,128)(2,1)} %collective-permute-done.25.refs_1_), custom_call_target="tpu_custom_call" | custom-call | flops 1000 | bytes 1000 | tf_op jit(solution)/shard_map/pallas_call | solution.py:336
  263.3 1.9 collective-permute-start.28
  270.9 1.4 stack.50
  274.2 7.3 %collective-permute-done.28.refs_1_ = bf16[256,2048]{1,0:T(8,128)(2,1)} collective-permute-done((bf16[256,2048]{1,0:T(8,128)(2,1)}, bf16[256,2048]{1,0:T(8,128)(2,1)}, u32[]{:S(2)}, u32[]{:S(2)}) %collective-permute-start.28) | collective-permute-done | bytes 1048608 | tf_op jit(solution)/shard_map/ppermute | solution.py:33
  281.5 2.4 shard_map.205
  284.0 2.4 copy.68
  286.4 6.3 %collective-permute-done.29.right_ref = bf16[1152,512]{1,0:T(8,128)(2,1)S(1)} collective-permute-done((bf16[1152,512]{1,0:T(8,128)(2,1)}, bf16[1152,512]{1,0:T(8,128)(2,1)S(1)}, u32[]{:S(2)}, u32[]{:S(2)}) %collective-permute-start.29) | collective-permute-done | bytes 1179680 | tf_op jit(solution)/shard_map/ppermute | solution.py:69
  292.7 3.9 %collective-permute-done.30.left_ref = bf16[1152,512]{1,0:T(8,128)(2,1)S(1)} collective-permute-done((bf16[1152,512]{1,0:T(8,128)(2,1)S(1)}, bf16[1152,512]{1,0:T(8,128)(2,1)S(1)}, u32[]{:S(2)}, u32[]{:S(2)}) %collective-permute-start.30) | collective-permute-done | bytes 1179680 | tf_op jit(solution)/shard_map/ppermute | solution.py:70
  297.6 4.0 %shard_map.206 = (f32[1,512,384]{2,1,0:T(8,128)}, f32[1,512,384]{2,1,0:T(8,128)}, f32[1,512,384]{2,1,0:T(8,128)}) custom-call(s32[1]{0:T(128)} %bitcast.2.flag_ref, bf16[1152,512]{1,0:T(8,128)(2,1)} %get-tuple-element.224.mine_ref, bf16[1152,512]{1,0:T(8,128)(2,1)} %copy-done.4, bf16[1152,512]{1,0:T(8,128)(2,1)} %copy-done.5, bf16[3,384,512]{2,1,0:T(8,128)(2,1)} %bitcast.47), custom_call_target="tpu_custom_call" | custom-call | tf_op jit(solution)/shard_map/pallas_call | solution.py:369
  (130 shorter events, 26.6 us)
Async XLA Ops:
  7.2 247.4 %reduce-scatter.2.cloned.1.call-start = ((), (), s32[]{:S(2)}) async-start(), calls=%async_computation.1 | async-start | bytes 737280 | tf_op jit(solution)/shard_map/reduce_scatter | solution.py:542
  7.2 27.3 %collective-permute-start = (bf16[256,2048]{1,0:T(8,128)(2,1)}, bf16[256,2048]{1,0:T(8,128)(2,1)S(1)}, u32[]{:S(2)}, u32[]{:S(2)}) collective-permute-start(bf16[256,2048]{1,0:T(8,128)(2,1)} %param.15), channel_id=1, source_target_pairs={{0,2},{1,5},{2,0},{3,7},{4,6},{5,1},{6,4},{7,3},{8,10},{9,13},{10,... | collective-permute-start | bytes 3145736 | tf_op jit(solution)/shard_map/ppermute | solution.py:33
  10.2 24.3 %collective-permute-start.1 = (bf16[256,2048]{1,0:T(8,128)(2,1)}, bf16[256,2048]{1,0:T(8,128)(2,1)S(1)}, u32[]{:S(2)}, u32[]{:S(2)}) collective-permute-start(bf16[256,2048]{1,0:T(8,128)(2,1)} %param.21), channel_id=1, source_target_pairs={{0,2},{1,5},{2,0},{3,7},{4,6},{5,1},{6,4},{7,3},{8,10},{9,13},{10,... | collective-permute-start | bytes 3145736 | tf_op jit(solution)/shard_map/ppermute | solution.py:33
  12.9 5.4 %copy-start.10 = (s32[256,4]{0,1:T(4,128)S(1)}, s32[256,4]{0,1:T(4,128)}, u32[]{:S(2)}) copy-start(s32[256,4]{0,1:T(4,128)} %param.16) | copy-start | bytes 12292
  12.9 5.4 %copy-start.11 = (f32[256,4]{0,1:T(4,128)S(1)}, f32[256,4]{0,1:T(4,128)}, u32[]{:S(2)}) copy-start(f32[256,4]{0,1:T(4,128)} %param.17) | copy-start | bytes 12292
  18.3 26.7 %copy-start.6 = (bf16[256,2048]{1,0:T(8,128)(2,1)S(1)}, bf16[256,2048]{1,0:T(8,128)(2,1)}, u32[]{:S(2)}) copy-start(bf16[256,2048]{1,0:T(8,128)(2,1)} %param.15) | copy-start | bytes 3145732
  18.3 2.3 collective-permute-start.3
  18.3 16.2 %collective-permute-start.2 = (f32[8,256]{1,0:T(8,128)S(1)}, f32[8,256]{1,0:T(8,128)S(1)}, u32[]{:S(2)}, u32[]{:S(2)}) collective-permute-start(f32[8,256]{1,0:T(8,128)S(1)} %bitcast.66), channel_id=1, source_target_pairs={{0,2},{1,5},{2,0},{3,7},{4,6},{5,1},{6,4},{7,3},{8,10},{9,13},{10,... | collective-permute-start | bytes 24584 | tf_op jit(solution)/shard_map/ppermute | solution.py:33
  34.5 8.6 %copy-start.7 = (bf16[256,2048]{1,0:T(8,128)(2,1)}, bf16[256,2048]{1,0:T(8,128)(2,1)S(1)}, u32[]{:S(2)}) copy-start(bf16[256,2048]{1,0:T(8,128)(2,1)S(1)} %collective-permute-done) | copy-start | bytes 3145732
  34.5 8.6 %copy-start.8 = (bf16[256,2048]{1,0:T(8,128)(2,1)}, bf16[256,2048]{1,0:T(8,128)(2,1)S(1)}, u32[]{:S(2)}) copy-start(bf16[256,2048]{1,0:T(8,128)(2,1)S(1)} %collective-permute-done.1) | copy-start | bytes 3145732
  34.6 8.4 %collective-permute-start.5 = (bf16[3,2,48,512]{3,2,1,0:T(8,128)(2,1)S(1)}, bf16[3,2,48,512]{3,2,1,0:T(8,128)(2,1)S(1)}, u32[]{:S(2)}, u32[]{:S(2)}) collective-permute-start(bf16[3,2,48,512]{3,2,1,0:T(8,128)(2,1)S(1)} %dynamic-slice_bitcast_fusion.1), channel_id=1, source_target_pairs={{0,2},{1,3},{2,0},{3,1},{4,6},{5,7},{6,4},{7,5},{8,10},{9,11},{10,... | collective-permute-start | bytes 884744 | tf_op jit(solution)/shard_map/ppermute | solution.py:33
  37.3 11.2 %collective-permute-start.4 = (f32[8,512]{1,0:T(8,128)S(1)}, f32[8,512]{1,0:T(8,128)S(1)}, u32[]{:S(2)}, u32[]{:S(2)}) collective-permute-start(f32[8,512]{1,0:T(8,128)S(1)} %pad_maximum_fusion.4), channel_id=1, source_target_pairs={{0,4},{1,3},{2,6},{3,1},{4,0},{5,7},{6,2},{7,5},{8,12},{9,11},{10,... | collective-permute-start | bytes 49160 | tf_op jit(solution)/shard_map/ppermute | solution.py:33
  43.1 5.4 %collective-permute-start.6 = (bf16[3,1,48,512]{3,2,1,0:T(8,128)(2,1)S(1)}, bf16[3,1,48,512]{3,2,1,0:T(8,128)(2,1)S(1)}, u32[]{:S(2)}, u32[]{:S(2)}) collective-permute-start(bf16[3,1,48,512]{3,2,1,0:T(8,128)(2,1)S(1)} %constant_dynamic-slice_fusion.15), channel_id=1, source_target_pairs={{0,4},{1,5},{2,6},{3,7},{4,0},{5,1},{6,2},{7,3},{8,12},{9,13},{10,... | collective-permute-start | bytes 442376 | tf_op jit(solution)/shard_map/ppermute | solution.py:33
  48.5 26.5 %copy-start = (bf16[512,2048]{1,0:T(8,128)(2,1)}, bf16[512,2048]{1,0:T(8,128)(2,1)S(1)}, u32[]{:S(2)}) copy-start(bf16[512,2048]{1,0:T(8,128)(2,1)S(1)} %get-tuple-element.135.a_ref.xa_ref) | copy-start | bytes 6291460
  48.6 4.1 %collective-permute-start.10 = (f32[8,1024]{1,0:T(8,128)S(1)}, f32[8,1024]{1,0:T(8,128)S(1)}, u32[]{:S(2)}, u32[]{:S(2)}) collective-permute-start(f32[8,1024]{1,0:T(8,128)S(1)} %constant_dynamic-update-slice_fusion), channel_id=1, source_target_pairs={{0,1},{1,0},{2,3},{3,2},{4,5},{5,4},{6,7},{7,6},{8,9},{9,8},{10,11... | collective-permute-start | bytes 98312 | tf_op jit(solution)/shard_map/ppermute | solution.py:33
  49.3 36.1 %collective-permute-start.9 = (bf16[512,2048]{1,0:T(8,128)(2,1)S(1)}, bf16[512,2048]{1,0:T(8,128)(2,1)}, u32[]{:S(2)}, u32[]{:S(2)}) collective-permute-start(bf16[512,2048]{1,0:T(8,128)(2,1)S(1)} %get-tuple-element.135.a_ref.xa_ref), channel_id=1, source_target_pairs={{0,1},{1,0},{2,3},{3,2},{4,5},{5,4},{6,7},{7,6},{8,9},{9,8},{10,11... | collective-permute-start | bytes 6291464 | tf_op jit(solution)/shard_map/ppermute | solution.py:33
  49.9 62.3 %collective-permute-start.7 = (bf16[512,2048]{1,0:T(8,128)(2,1)S(1)}, bf16[512,2048]{1,0:T(8,128)(2,1)}, u32[]{:S(2)}, u32[]{:S(2)}) collective-permute-start(bf16[512,2048]{1,0:T(8,128)(2,1)S(1)} %get-tuple-element.135.a_ref.xa_ref), channel_id=1, source_target_pairs={{0,4},{1,3},{2,6},{3,1},{4,0},{5,7},{6,2},{7,5},{8,12},{9,11},{10,... | collective-permute-start | bytes 6291464 | tf_op jit(solution)/shard_map/ppermute | solution.py:33
  51.4 47.1 %collective-permute-start.13 = (bf16[512,2048]{1,0:T(8,128)(2,1)}, bf16[512,2048]{1,0:T(8,128)(2,1)}, u32[]{:S(2)}, u32[]{:S(2)}) collective-permute-start(bf16[512,2048]{1,0:T(8,128)(2,1)} %get-tuple-element.138.a_ref.ca_ref), channel_id=1, source_target_pairs={{0,1},{1,0},{2,3},{3,2},{4,5},{5,4},{6,7},{7,6},{8,9},{9,8},{10,11... | collective-permute-start | bytes 6291464 | tf_op jit(solution)/shard_map/ppermute | solution.py:33
  51.4 60.8 %collective-permute-start.8 = (bf16[512,2048]{1,0:T(8,128)(2,1)}, bf16[512,2048]{1,0:T(8,128)(2,1)}, u32[]{:S(2)}, u32[]{:S(2)}) collective-permute-start(bf16[512,2048]{1,0:T(8,128)(2,1)} %get-tuple-element.138.a_ref.ca_ref), channel_id=1, source_target_pairs={{0,4},{1,3},{2,6},{3,1},{4,0},{5,7},{6,2},{7,5},{8,12},{9,11},{10,... | collective-permute-start | bytes 6291464 | tf_op jit(solution)/shard_map/ppermute | solution.py:33
  52.7 6.2 %collective-permute-start.11 = (bf16[1,144,512]{2,1,0:T(8,128)(2,1)S(1)}, bf16[1,144,512]{2,1,0:T(8,128)(2,1)S(1)}, u32[]{:S(2)}, u32[]{:S(2)}) collective-permute-start(bf16[1,144,512]{2,1,0:T(8,128)(2,1)S(1)} %bitcast.57), channel_id=1, source_target_pairs={{0,8},{8,0},{16,24},{24,16},{1,9},{9,1},{17,25},{25,17},{2,10},{10... | collective-permute-start | bytes 442376 | tf_op jit(solution)/shard_map/ppermute | solution.py:78
  59.0 16.0 %collective-permute-start.12 = (bf16[2,144,512]{2,1,0:T(8,128)(2,1)S(1)}, bf16[2,144,512]{2,1,0:T(8,128)(2,1)S(1)}, u32[]{:S(2)}, u32[]{:S(2)}) collective-permute-start(bf16[2,144,512]{2,1,0:T(8,128)(2,1)S(1)} %pad_maximum_fusion.3), channel_id=1, source_target_pairs={{0,16},{8,24},{16,0},{24,8},{1,17},{9,25},{17,1},{25,9},{2,18},{10... | collective-permute-start | bytes 884744 | tf_op jit(solution)/shard_map/ppermute | solution.py:78
  112.2 12.0 %collective-permute-start.14 = (bf16[512,2048]{1,0:T(8,128)(2,1)}, bf16[512,2048]{1,0:T(8,128)(2,1)S(1)}, u32[]{:S(2)}, u32[]{:S(2)}) collective-permute-start(bf16[512,2048]{1,0:T(8,128)(2,1)} %collective-permute-done.7.a_ref.xa_ref), channel_id=1, source_target_pairs={{0,1},{1,0},{2,3},{3,2},{4,5},{5,4},{6,7},{7,6},{8,9},{9,8},{10,11... | collective-permute-start | bytes 6291464 | tf_op jit(solution)/shard_map/ppermute | solution.py:33
  112.3 12.0 %collective-permute-start.15 = (bf16[512,2048]{1,0:T(8,128)(2,1)}, bf16[512,2048]{1,0:T(8,128)(2,1)}, u32[]{:S(2)}, u32[]{:S(2)}) collective-permute-start(bf16[512,2048]{1,0:T(8,128)(2,1)} %collective-permute-done.8.a_ref.ca_ref), channel_id=1, source_target_pairs={{0,1},{1,0},{2,3},{3,2},{4,5},{5,4},{6,7},{7,6},{8,9},{9,8},{10,11... | collective-permute-start | bytes 6291464 | tf_op jit(solution)/shard_map/ppermute | solution.py:33
  124.3 1.4 copy-start.1
  124.3 46.5 %collective-permute-start.18 = (bf16[512,2048]{1,0:T(8,128)(2,1)}, bf16[512,2048]{1,0:T(8,128)(2,1)}, u32[]{:S(2)}, u32[]{:S(2)}) collective-permute-start(bf16[512,2048]{1,0:T(8,128)(2,1)} %get-tuple-element.162), channel_id=1, source_target_pairs={{0,1},{1,0},{2,3},{3,2},{4,5},{5,4},{6,7},{7,6},{8,9},{9,8},{10,11... | collective-permute-start | bytes 6291464 | tf_op jit(solution)/shard_map/ppermute | solution.py:33
  124.4 46.4 %collective-permute-start.19 = (bf16[512,2048]{1,0:T(8,128)(2,1)}, bf16[512,2048]{1,0:T(8,128)(2,1)}, u32[]{:S(2)}, u32[]{:S(2)}) collective-permute-start(bf16[512,2048]{1,0:T(8,128)(2,1)} %get-tuple-element.164), channel_id=1, source_target_pairs={{0,1},{1,0},{2,3},{3,2},{4,5},{5,4},{6,7},{7,6},{8,9},{9,8},{10,11... | collective-permute-start | bytes 6291464 | tf_op jit(solution)/shard_map/ppermute | solution.py:33
  152.4 18.5 %collective-permute-start.17 = (bf16[512,2048]{1,0:T(8,128)(2,1)}, bf16[512,2048]{1,0:T(8,128)(2,1)S(1)}, u32[]{:S(2)}, u32[]{:S(2)}) collective-permute-start(bf16[512,2048]{1,0:T(8,128)(2,1)} %get-tuple-element.158), channel_id=1, source_target_pairs={{0,1},{1,0},{2,3},{3,2},{4,5},{5,4},{6,7},{7,6},{8,9},{9,8},{10,11... | collective-permute-start | bytes 6291464 | tf_op jit(solution)/shard_map/ppermute | solution.py:33
  152.5 18.4 %collective-permute-start.16 = (bf16[512,2048]{1,0:T(8,128)(2,1)}, bf16[512,2048]{1,0:T(8,128)(2,1)}, u32[]{:S(2)}, u32[]{:S(2)}) collective-permute-start(bf16[512,2048]{1,0:T(8,128)(2,1)} %get-tuple-element.156), channel_id=1, source_target_pairs={{0,1},{1,0},{2,3},{3,2},{4,5},{5,4},{6,7},{7,6},{8,9},{9,8},{10,11... | collective-permute-start | bytes 6291464 | tf_op jit(solution)/shard_map/ppermute | solution.py:33
  170.8 9.7 %copy-start.3 = (bf16[512,2048]{1,0:T(8,128)(2,1)}, bf16[512,2048]{1,0:T(8,128)(2,1)S(1)}, u32[]{:S(2)}) copy-start(bf16[512,2048]{1,0:T(8,128)(2,1)S(1)} %collective-permute-done.17.refs_1_) | copy-start | bytes 6291460
  170.9 36.0 %collective-permute-start.20 = (bf16[1152,512]{1,0:T(8,128)(2,1)}, bf16[1152,512]{1,0:T(8,128)(2,1)}, u32[]{:S(2)}, u32[]{:S(2)}) collective-permute-start(bf16[1152,512]{1,0:T(8,128)(2,1)} %get-tuple-element.171), channel_id=1, source_target_pairs={{0,8},{1,9},{2,10},{3,11},{4,12},{5,13},{6,14},{7,15}} | collective-permute-start | bytes 3538952 | tf_op jit(solution)/shard_map/ppermute | solution.py:69
  174.4 32.5 %collective-permute-start.21 = (bf16[1152,512]{1,0:T(8,128)(2,1)S(1)}, bf16[1152,512]{1,0:T(8,128)(2,1)}, u32[]{:S(2)}, u32[]{:S(2)}) collective-permute-start(bf16[1152,512]{1,0:T(8,128)(2,1)S(1)} %get-tuple-element.172), channel_id=1, source_target_pairs={{24,16},{25,17},{26,18},{27,19},{28,20},{29,21},{30,22},{31,23}} | collective-permute-start | bytes 3538952 | tf_op jit(solution)/shard_map/ppermute | solution.py:70
  180.5 15.1 %collective-permute-start.22 = (bf16[256,2048]{1,0:T(8,128)(2,1)}, bf16[256,2048]{1,0:T(8,128)(2,1)}, u32[]{:S(2)}, u32[]{:S(2)}) collective-permute-start(bf16[256,2048]{1,0:T(8,128)(2,1)} %get-tuple-element.175), channel_id=1, source_target_pairs={{0,4},{1,3},{2,6},{3,1},{4,0},{5,7},{6,2},{7,5},{8,12},{9,11},{10,... | collective-permute-start | bytes 3145736 | tf_op jit(solution)/shard_map/ppermute | solution.py:33
  180.7 26.1 %collective-permute-start.23 = (bf16[256,2048]{1,0:T(8,128)(2,1)}, bf16[256,2048]{1,0:T(8,128)(2,1)}, u32[]{:S(2)}, u32[]{:S(2)}) collective-permute-start(bf16[256,2048]{1,0:T(8,128)(2,1)} %get-tuple-element.176), channel_id=1, source_target_pairs={{0,4},{1,3},{2,6},{3,1},{4,0},{5,7},{6,2},{7,5},{8,12},{9,11},{10,... | collective-permute-start | bytes 3145736 | tf_op jit(solution)/shard_map/ppermute | solution.py:33
  195.5 15.4 %copy-start.2 = (bf16[512,2048]{1,0:T(8,128)(2,1)S(1)}, bf16[512,2048]{1,0:T(8,128)(2,1)}, u32[]{:S(2)}) copy-start(bf16[512,2048]{1,0:T(8,128)(2,1)} %shard_map.198) | copy-start | bytes 6291460
  210.9 43.7 %collective-permute-start.25 = (bf16[512,2048]{1,0:T(8,128)(2,1)S(1)}, bf16[512,2048]{1,0:T(8,128)(2,1)}, u32[]{:S(2)}, u32[]{:S(2)}) collective-permute-start(bf16[512,2048]{1,0:T(8,128)(2,1)S(1)} %copy-done.2), channel_id=1, source_target_pairs={{0,4},{1,3},{2,6},{3,1},{4,0},{5,7},{6,2},{7,5},{8,12},{9,11},{10,... | collective-permute-start | bytes 6291464 | tf_op jit(solution)/shard_map/ppermute | solution.py:33
  213.1 8.8 %copy-start.13 = (s32[8]{0:T(128)S(1)}, s32[8]{0:T(128)}, u32[]{:S(2)}) copy-start(s32[8]{0:T(128)} %constant.132.clone) | copy-start | bytes 100
  213.1 12.0 %copy-start.12 = (s32[8]{0:T(128)S(1)}, s32[8]{0:T(128)}, u32[]{:S(2)}) copy-start(s32[8]{0:T(128)} %constant.131.clone) | copy-start | bytes 100
  213.1 70.9 %all-gather.5.cloned.1.call-start = ((), (), s32[]{:S(2)}) async-start(), calls=%async_computation.2 | async-start | bytes 1327104 | tf_op jit(solution)/shard_map/all_gather | solution.py:562
  213.1 41.5 %collective-permute-start.26 = (bf16[1152,512]{1,0:T(8,128)(2,1)}, bf16[1152,512]{1,0:T(8,128)(2,1)}, u32[]{:S(2)}, u32[]{:S(2)}) collective-permute-start(bf16[1152,512]{1,0:T(8,128)(2,1)} %get-tuple-element.192), channel_id=1, source_target_pairs={{0,8},{8,16},{1,9},{9,17},{2,10},{10,18},{3,11},{11,19},{4,12},{12... | collective-permute-start | bytes 3538952 | tf_op jit(solution)/shard_map/ppermute | solution.py:69
  215.4 39.1 %collective-permute-start.27 = (bf16[1152,512]{1,0:T(8,128)(2,1)S(1)}, bf16[1152,512]{1,0:T(8,128)(2,1)}, u32[]{:S(2)}, u32[]{:S(2)}) collective-permute-start(bf16[1152,512]{1,0:T(8,128)(2,1)S(1)} %get-tuple-element.193), channel_id=1, source_target_pairs={{24,16},{16,8},{25,17},{17,9},{26,18},{18,10},{27,19},{19,11},{28,... | collective-permute-start | bytes 3538952 | tf_op jit(solution)/shard_map/ppermute | solution.py:70
  221.8 30.4 %collective-permute-start.24 = (bf16[256,2048]{1,0:T(8,128)(2,1)}, bf16[256,2048]{1,0:T(8,128)(2,1)}, u32[]{:S(2)}, u32[]{:S(2)}) collective-permute-start(bf16[256,2048]{1,0:T(8,128)(2,1)} %get-tuple-element.187), channel_id=1, source_target_pairs={{0,2},{1,5},{2,0},{3,7},{4,6},{5,1},{6,4},{7,3},{8,10},{9,13},{10,... | collective-permute-start | bytes 3145736 | tf_op jit(solution)/shard_map/ppermute | solution.py:33
  258.7 9.1 %copy-start.9 = (f32[8,2,2048]{2,1,0:T(2,128)S(1)}, f32[8,2,2048]{2,1,0:T(2,128)}, u32[]{:S(2)}) copy-start(f32[8,2,2048]{2,1,0:T(2,128)} %all-gather.2) | copy-start | bytes 393220
  263.3 18.3 %collective-permute-start.28 = (bf16[256,2048]{1,0:T(8,128)(2,1)}, bf16[256,2048]{1,0:T(8,128)(2,1)}, u32[]{:S(2)}, u32[]{:S(2)}) collective-permute-start(bf16[256,2048]{1,0:T(8,128)(2,1)} %get-tuple-element.202), channel_id=1, source_target_pairs={{0,2},{1,5},{2,0},{3,7},{4,6},{5,1},{6,4},{7,3},{8,10},{9,13},{10,... | collective-permute-start | bytes 3145736 | tf_op jit(solution)/shard_map/ppermute | solution.py:33
  265.2 27.5 %collective-permute-start.29 = (bf16[1152,512]{1,0:T(8,128)(2,1)}, bf16[1152,512]{1,0:T(8,128)(2,1)S(1)}, u32[]{:S(2)}, u32[]{:S(2)}) collective-permute-start(bf16[1152,512]{1,0:T(8,128)(2,1)} %get-tuple-element.204), channel_id=1, source_target_pairs={{0,8},{8,16},{16,24},{1,9},{9,17},{17,25},{2,10},{10,18},{18,26},{... | collective-permute-start | bytes 3538952 | tf_op jit(solution)/shard_map/ppermute | solution.py:69
  266.5 30.0 %collective-permute-start.30 = (bf16[1152,512]{1,0:T(8,128)(2,1)S(1)}, bf16[1152,512]{1,0:T(8,128)(2,1)S(1)}, u32[]{:S(2)}, u32[]{:S(2)}) collective-permute-start(bf16[1152,512]{1,0:T(8,128)(2,1)S(1)} %get-tuple-element.205), channel_id=1, source_target_pairs={{24,16},{16,8},{8,0},{25,17},{17,9},{9,1},{26,18},{18,10},{10,2},{... | collective-permute-start | bytes 3538952 | tf_op jit(solution)/shard_map/ppermute | solution.py:70
  292.7 3.9 %copy-start.4 = (bf16[1152,512]{1,0:T(8,128)(2,1)}, bf16[1152,512]{1,0:T(8,128)(2,1)S(1)}, u32[]{:S(2)}) copy-start(bf16[1152,512]{1,0:T(8,128)(2,1)S(1)} %collective-permute-done.29.right_ref) | copy-start | bytes 3538948
  296.5 1.0 copy-start.5
Sparse Core Ops, SparseCore 0:
  213.2 28.2 reduce-scatter.1
  254.8 25.5 all-gather.4

commit v3 on v2

--- a/solution.py
+++ b/solution.py
@@ -96,7 +96,7 @@
 
 
 def tile_of(rows):
-    tile = min(rows, 256)
+    tile = min(rows, 512)
     assert rows % tile == 0
     return tile
 

time: 310 us -> 312 us (level)
  no operation moved by 1% of the time
where the time goes in v3:
time: 312 us; the launch traced here: 311 us
  Pallas kernels  128 us (41%)
  waiting for transfers between devices  62.6 us (20%)
  starting transfers between devices  36 us (12%)
  other arithmetic  21.4 us (7%)
  blocking collectives  21.3 us (7%)
  local copies, waits for them, and re-layouts  20.9 us (7%)
  between operations  20.2 us (6%)
    ppermute x23, waiting for transfers between devices, flip(): return lax.ppermute(value, 'expert', pairs)  35.6 us
    pallas_call x2, Pallas kernels, backward(): call(body, (2 * tiles,), [first_rows(tile, width, tiles), second_rows(til...  29.8 us
    pallas_call x2, Pallas kernels, forward(): call(body, (2 * tiles,), [first_rows(tile, width, tiles), second_rows(til...  28.1 us
    all_gather x1, blocking collectives, per_device(): dots = lax.all_gather(jnp.concatenate([d_near, d_far]).T, 'expert', axis=0)  21.3 us
    ppermute x23, starting transfers between devices, flip(): return lax.ppermute(value, 'expert', pairs)  19.9 us
    pallas_call x5, Pallas kernels, sum_of(): call(body, (rows // tile,), [by_rows(tile, width)] * len(arrays), by_rows...  17.8 us
    ppermute x2, waiting for transfers between devices, line_gather(): lax.ppermute(found, 'dp', [(i, i ^ bit) for i in range(groups)])  16.7 us
    pallas_call x1, Pallas kernels, weight_totals(): call(body, (width // tile,), [whole(pre.shape), cut, cut, whole(hidden.sh...  14.1 us
  transfers between devices with their start and end apart: 33, of which 10 were waited for; matrix products, arithmetic and copies ran while one was open for 12% of the time, Pallas kernels for 40%

profile of v3, /device:TPU:0, one launch (start us, length us, event | category | flops | bytes accessed | tf_op | source)
XLA Modules:
  0.0 310.8 jit_solution(3150578621821642803)
XLA Ops:
  7.2 3.0 collective-permute-start
  12.9 3.5 %shard_map.190 = bf16[3,384,512]{2,1,0:T(8,128)(2,1)} custom-call(s32[2]{0:T(128)} %pad_add_fusion.scalar_ref, bf16[2048,384]{1,0:T(8,128)(2,1)} %bitcast.41, bf16[2048,384]{1,0:T(8,128)(2,1)} %bitcast.43, bf16[2048,384]{1,0:T(8,128)(2,1)} %bitcast.45), custom_call_target="tpu_custom_call" | custom-call | flops 1000 | bytes 1000 | tf_op jit(solution)/shard_map/pallas_call | solution.py:395
  16.4 1.9 dynamic-slice_bitcast_fusion
  18.3 2.0 collective-permute-start.2
  21.9 12.6 %collective-permute-done.2 = f32[8,256]{1,0:T(8,128)S(1)} collective-permute-done((f32[8,256]{1,0:T(8,128)S(1)}, f32[8,256]{1,0:T(8,128)S(1)}, u32[]{:S(2)}, u32[]{:S(2)}) %collective-permute-start.2) | collective-permute-done | bytes 8224 | tf_op jit(solution)/shard_map/ppermute | solution.py:33
  34.6 2.1 collective-permute-start.5
  37.3 1.5 collective-permute-start.4
  38.9 4.2 %collective-permute-done.5 = bf16[3,2,48,512]{3,2,1,0:T(8,128)(2,1)S(1)} collective-permute-done((bf16[3,2,48,512]{3,2,1,0:T(8,128)(2,1)S(1)}, bf16[3,2,48,512]{3,2,1,0:T(8,128)(2,1)S(1)}, u32[]{:S(2)}, u32[]{:S(2)}) %collective-permute-start.5) | collective-permute-done | bytes 294944 | tf_op jit(solution)/shard_map/ppermute | solution.py:33
  43.1 1.8 collective-permute-start.6
  44.9 3.6 %pad_maximum_fusion = (bf16[512,2048]{1,0:T(8,128)(2,1)S(1)}, bf16[512,2048]{1,0:T(8,128)(2,1)}) fusion(bf16[256,2048]{1,0:T(8,128)(2,1)} %copy-done.7, bf16[256,2048]{1,0:T(8,128)(2,1)S(1)} %copy-done.6, bf16[256,2048]{1,0:T(8,128)(2,1)} %copy-done.8, bf16[256,2048]{1,0:T(8,128)(2,1)} %param.21), kind=kLoop, calls=%fused_computation.9 | loop fusion | flops 8388608 | bytes 8388608 | tf_op jit(solution)/shard_map/concatenate | solution.py:19
  49.9 1.5 collective-permute-start.7
  52.7 1.6 collective-permute-start.11
  55.5 3.4 %collective-permute-done.11 = bf16[1,144,512]{2,1,0:T(8,128)(2,1)S(1)} collective-permute-done((bf16[1,144,512]{2,1,0:T(8,128)(2,1)S(1)}, bf16[1,144,512]{2,1,0:T(8,128)(2,1)S(1)}, u32[]{:S(2)}, u32[]{:S(2)}) %collective-permute-start.11) | collective-permute-done | bytes 147488 | tf_op jit(solution)/shard_map/ppermute | solution.py:78
  59.0 2.7 collective-permute-start.12
  61.6 13.3 %collective-permute-done.12 = bf16[2,144,512]{2,1,0:T(8,128)(2,1)S(1)} collective-permute-done((bf16[2,144,512]{2,1,0:T(8,128)(2,1)S(1)}, bf16[2,144,512]{2,1,0:T(8,128)(2,1)S(1)}, u32[]{:S(2)}, u32[]{:S(2)}) %collective-permute-start.12) | collective-permute-done | bytes 294944 | tf_op jit(solution)/shard_map/ppermute | solution.py:78
  77.4 6.0 %shard_map.191 = (bf16[2048,1024]{1,0:T(8,128)(2,1)}, bf16[2048,512]{1,0:T(8,128)(2,1)}) custom-call(bf16[2048,384]{1,0:T(8,128)(2,1)} %bitcast.42, bf16[2048,384]{1,0:T(8,128)(2,1)} %bitcast.44, bf16[2048,384]{1,0:T(8,128)(2,1)} %bitcast.46, bf16[3,128,2048]{2,1,0:T(8,128)(2,1)} %fusion.6.hot_ref), custom_call_target="tpu_custom_call" | custom-call | flops 1000 | bytes 1000 | tf_op jit(solution)/shard_map/pallas_call | solution.py:424
  83.4 14.0 %shard_map.192 = (f32[1024,1024]{1,0:T(8,128)}, bf16[512,1024]{1,0:T(8,128)(2,1)}, bf16[512,2048]{1,0:T(8,128)(2,1)}, bf16[512,2048]{1,0:T(8,128)(2,1)}) custom-call(bf16[512,2048]{1,0:T(8,128)(2,1)} %copy-done, bf16[512,2048]{1,0:T(8,128)(2,1)} %collective-permute-done.9.b_ref.xb_ref, f32[1024,2]{1,0:T(8,128)} %bitcast.52, ...), custom_call_target="tpu_custom_call" | custom-call | flops 1000 | bytes 1000 | tf_op jit(solution)/shard_map/pallas_call | solution.py:169
  97.4 14.9 %shard_map.193 = (bf16[1024,1024]{1,0:T(8,128)(2,1)}, bf16[512,2048]{1,0:T(8,128)(2,1)}, bf16[512,2048]{1,0:T(8,128)(2,1)}, f32[1024,2]{1,0:T(8,128)}) custom-call(bf16[512,2048]{1,0:T(8,128)(2,1)} %get-tuple-element.138.a_ref.ca_ref, bf16[512,2048]{1,0:T(8,128)(2,1)} %collective-permute-done.13.b_ref.cb_ref, f32[1024,1024]{1,0:T(8,128)} %get-tuple-element.122.act_ref, ...), custom_call_target="tpu_custom_call" | custom-call | flops 1000 | bytes 1000 | tf_op jit(solution)/shard_map/pallas_call | solution.py:220
  112.9 11.5 %shard_map.194 = (f32[1024,2048]{1,0:T(8,128)}, f32[512,2048]{1,0:T(8,128)}) custom-call(bf16[1024,1024]{1,0:T(8,128)(2,1)} %get-tuple-element.134.pre_ref, bf16[512,2048]{1,0:T(8,128)(2,1)} %copy-done, bf16[512,2048]{1,0:T(8,128)(2,1)} %collective-permute-done.9.b_ref.xb_ref, bf16[512,1024]{1,0:T(8,128)(2,1)} %get-tuple-element.137.hidden_ref, ...), custom_call_target="tpu_custom_call" | custom-call | flops 1000 | bytes 1000 | tf_op jit(solution)/shard_map/pallas_call | solution.py:249
  125.7 14.1 %shard_map.195 = (f32[1024,1024]{1,0:T(8,128)}, bf16[512,1024]{1,0:T(8,128)(2,1)}, bf16[512,2048]{1,0:T(8,128)(2,1)}, bf16[512,2048]{1,0:T(8,128)(2,1)}) custom-call(bf16[512,2048]{1,0:T(8,128)(2,1)} %collective-permute-done.7.a_ref.xa_ref, bf16[512,2048]{1,0:T(8,128)(2,1)} %copy-done.1, f32[1024,2]{1,0:T(8,128)} %bitcast.50, ...), custom_call_target="tpu_custom_call" | custom-call | flops 1000 | bytes 1000 | tf_op jit(solution)/shard_map/pallas_call | solution.py:169
  139.8 14.9 %shard_map.196 = (bf16[1024,1024]{1,0:T(8,128)(2,1)}, bf16[512,2048]{1,0:T(8,128)(2,1)}, bf16[512,2048]{1,0:T(8,128)(2,1)}, f32[1024,2]{1,0:T(8,128)}) custom-call(bf16[512,2048]{1,0:T(8,128)(2,1)} %collective-permute-done.8.a_ref.ca_ref, bf16[512,2048]{1,0:T(8,128)(2,1)} %collective-permute-done.15.b_ref.cb_ref, f32[1024,1024]{1,0:T(8,128)} %get-tuple-element.149.act_ref, ...), custom_call_target="tpu_custom_call" | custom-call | flops 1000 | bytes 1000 | tf_op jit(solution)/shard_map/pallas_call | solution.py:220
  155.2 14.1 %shard_map.197 = (bf16[1152,2048]{1,0:T(8,128)(2,1)}, bf16[384,2048]{1,0:T(8,128)(2,1)}) custom-call(bf16[1024,1024]{1,0:T(8,128)(2,1)} %get-tuple-element.150.pre_ref, bf16[512,2048]{1,0:T(8,128)(2,1)} %collective-permute-done.7.a_ref.xa_ref, bf16[512,2048]{1,0:T(8,128)(2,1)} %copy-done.1, bf16[512,1024]{1,0:T(8,128)(2,1)} %get-tuple-element.151.hidden_ref, ...), custom_call_target="tpu_custom_call" | custom-call | flops 1000 | bytes 1000 | tf_op jit(solution)/shard_map/pallas_call | solution.py:284
  169.4 3.8 %constant_dynamic-slice_fusion = (bf16[1152,512]{1,0:T(8,128)(2,1)}, bf16[1152,512]{1,0:T(8,128)(2,1)S(1)}, bf16[1152,512]{1,0:T(8,128)(2,1)}) fusion(bf16[1152,2048]{1,0:T(8,128)(2,1)} %get-tuple-element.154, s32[]{:T(128)S(6)} %select_n.200, s32[]{:T(128)S(6)} %select_n.178, s32[]{:T(128)S(6)} %select_n.177), kind=kLoop, calls=%fused_computation.35 | loop fusion | bytes 7077900 | tf_op jit(solution)/shard_map/dynamic_slice | solution.py:58
  173.2 3.5 %collective-permute-start.20 = (bf16[1152,512]{1,0:T(8,128)(2,1)}, bf16[1152,512]{1,0:T(8,128)(2,1)}, u32[]{:S(2)}, u32[]{:S(2)}) collective-permute-start(bf16[1152,512]{1,0:T(8,128)(2,1)} %get-tuple-element.171), channel_id=1, source_target_pairs={{0,8},{1,9},{2,10},{3,11},{4,12},{5,13},{6,14},{7,15}} | collective-permute-start | bytes 3538952 | tf_op jit(solution)/shard_map/ppermute | solution.py:69
  176.7 1.7 collective-permute-start.21
  178.4 4.5 %shard_map.201 = (bf16[256,2048]{1,0:T(8,128)(2,1)}, bf16[256,2048]{1,0:T(8,128)(2,1)}) custom-call(bf16[512,2048]{1,0:T(8,128)(2,1)} %get-tuple-element.173.refs_0_, bf16[512,2048]{1,0:T(8,128)(2,1)} %collective-permute-done.16.refs_1_), custom_call_target="tpu_custom_call" | custom-call | flops 1000 | bytes 1000 | tf_op jit(solution)/shard_map/pallas_call | solution.py:336
  183.1 1.8 collective-permute-start.23
  184.9 4.3 %shard_map.198 = bf16[512,2048]{1,0:T(8,128)(2,1)} custom-call(bf16[512,2048]{1,0:T(8,128)(2,1)} %get-tuple-element.165.refs_0_, bf16[512,2048]{1,0:T(8,128)(2,1)} %copy-done.3), custom_call_target="tpu_custom_call" | custom-call | flops 1000 | bytes 1000 | tf_op jit(solution)/shard_map/pallas_call | solution.py:309
  189.2 4.3 %shard_map.199.refs_0_ = bf16[512,2048]{1,0:T(8,128)(2,1)} custom-call(bf16[512,2048]{1,0:T(8,128)(2,1)} %get-tuple-element.167.refs_0_, bf16[512,2048]{1,0:T(8,128)(2,1)} %collective-permute-done.18.refs_1_), custom_call_target="tpu_custom_call" | custom-call | flops 1000 | bytes 1000 | tf_op jit(solution)/shard_map/pallas_call | solution.py:309
  193.5 4.3 %shard_map.200.refs_0_ = bf16[512,2048]{1,0:T(8,128)(2,1)} custom-call(bf16[512,2048]{1,0:T(8,128)(2,1)} %get-tuple-element.169.refs_0_, bf16[512,2048]{1,0:T(8,128)(2,1)} %collective-permute-done.19.refs_1_), custom_call_target="tpu_custom_call" | custom-call | flops 1000 | bytes 1000 | tf_op jit(solution)/shard_map/pallas_call | solution.py:309
  198.0 11.2 %collective-permute-done.23.refs_2_ = bf16[256,2048]{1,0:T(8,128)(2,1)} collective-permute-done((bf16[256,2048]{1,0:T(8,128)(2,1)}, bf16[256,2048]{1,0:T(8,128)(2,1)}, u32[]{:S(2)}, u32[]{:S(2)}) %collective-permute-start.23) | collective-permute-done | bytes 1048608 | tf_op jit(solution)/shard_map/ppermute | solution.py:33
  209.2 4.0 %add_convert_fusion.2 = (bf16[1152,512]{1,0:T(8,128)(2,1)S(1)}, bf16[1152,512]{1,0:T(8,128)(2,1)}) fusion(bf16[1152,512]{1,0:T(8,128)(2,1)} %collective-permute-done.21, bf16[1152,2048]{1,0:T(8,128)(2,1)} %get-tuple-element.154, s32[]{:T(128)S(6)} %select_n.179, bf16[1152,512]{1,0:T(8,128)(2,1)} %collective-permute-done.20, s32[]{:T(128)S(6)} %select_n.176), kind=kLoop, calls=%fused_computation.7 | loop fusion | flops 4718592 | bytes 7077896 | tf_op jit(solution)/shard_map/convert_element_type | solution.py:15
  213.5 1.9 slice.76
  215.5 2.3 collective-permute-start.26
  217.8 1.7 collective-permute-start.27
  219.5 4.6 %shard_map.202 = (bf16[256,2048]{1,0:T(8,128)(2,1)}, bf16[256,2048]{1,0:T(8,128)(2,1)}) custom-call(bf16[512,2048]{1,0:T(8,128)(2,1)} %shard_map.199.refs_0_, bf16[256,2048]{1,0:T(8,128)(2,1)} %collective-permute-done.22.refs_1_, bf16[256,2048]{1,0:T(8,128)(2,1)} %collective-permute-done.23.refs_2_), custom_call_target="tpu_custom_call" | custom-call | flops 1000 | bytes 1000 | tf_op jit(solution)/shard_map/pallas_call | solution.py:336
  233.2 21.3 %all-gather.2 = f32[8,2,2048]{2,1,0:T(2,128)} all-gather(f32[1,2,2048]{2,1,0:T(2,128)S(1)} %maximum_bitcast_fusion), channel_id=2, replica_groups=mesh['dp'=4,'expert'=8] {'expert'}, dimensions={0}, use_global_device_ids=true | all-gather | bytes 147456 | tf_op jit(solution)/shard_map/all_gather | solution.py:552
  254.5 2.4 shard_map.203
  257.0 4.0 %add_convert_fusion = (bf16[1152,512]{1,0:T(8,128)(2,1)S(1)}, bf16[1152,512]{1,0:T(8,128)(2,1)}) fusion(bf16[1152,512]{1,0:T(8,128)(2,1)} %collective-permute-done.27, bf16[1152,2048]{1,0:T(8,128)(2,1)} %get-tuple-element.154, s32[]{:T(128)S(6)} %select_n.181, bf16[1152,512]{1,0:T(8,128)(2,1)} %collective-permute-done.26, s32[]{:T(128)S(6)} %select_n.180), kind=kLoop, calls=%fused_computation.5 | loop fusion | flops 4718592 | bytes 7077896 | tf_op jit(solution)/shard_map/convert_element_type | solution.py:15
  261.0 4.6 %shard_map.204 = (bf16[256,2048]{1,0:T(8,128)(2,1)}, bf16[256,2048]{1,0:T(8,128)(2,1)}) custom-call(bf16[512,2048]{1,0:T(8,128)(2,1)} %shard_map.200.refs_0_, bf16[512,2048]{1,0:T(8,128)(2,1)} %collective-permute-done.25.refs_1_), custom_call_target="tpu_custom_call" | custom-call | flops 1000 | bytes 1000 | tf_op jit(solution)/shard_map/pallas_call | solution.py:336
  265.6 1.9 collective-permute-start.28
  273.3 1.4 stack.50
  276.6 7.3 %collective-permute-done.28.refs_1_ = bf16[256,2048]{1,0:T(8,128)(2,1)} collective-permute-done((bf16[256,2048]{1,0:T(8,128)(2,1)}, bf16[256,2048]{1,0:T(8,128)(2,1)}, u32[]{:S(2)}, u32[]{:S(2)}) %collective-permute-start.28) | collective-permute-done | bytes 1048608 | tf_op jit(solution)/shard_map/ppermute | solution.py:33
  283.9 2.4 shard_map.205
  286.3 2.4 copy.68
  288.7 6.4 %collective-permute-done.29.right_ref = bf16[1152,512]{1,0:T(8,128)(2,1)S(1)} collective-permute-done((bf16[1152,512]{1,0:T(8,128)(2,1)}, bf16[1152,512]{1,0:T(8,128)(2,1)S(1)}, u32[]{:S(2)}, u32[]{:S(2)}) %collective-permute-start.29) | collective-permute-done | bytes 1179680 | tf_op jit(solution)/shard_map/ppermute | solution.py:69
  295.1 3.9 %collective-permute-done.30.left_ref = bf16[1152,512]{1,0:T(8,128)(2,1)S(1)} collective-permute-done((bf16[1152,512]{1,0:T(8,128)(2,1)S(1)}, bf16[1152,512]{1,0:T(8,128)(2,1)S(1)}, u32[]{:S(2)}, u32[]{:S(2)}) %collective-permute-start.30) | collective-permute-done | bytes 1179680 | tf_op jit(solution)/shard_map/ppermute | solution.py:70
  300.0 4.0 %shard_map.206 = (f32[1,512,384]{2,1,0:T(8,128)}, f32[1,512,384]{2,1,0:T(8,128)}, f32[1,512,384]{2,1,0:T(8,128)}) custom-call(s32[1]{0:T(128)} %bitcast.2.flag_ref, bf16[1152,512]{1,0:T(8,128)(2,1)} %get-tuple-element.224.mine_ref, bf16[1152,512]{1,0:T(8,128)(2,1)} %copy-done.4, bf16[1152,512]{1,0:T(8,128)(2,1)} %copy-done.5, bf16[3,384,512]{2,1,0:T(8,128)(2,1)} %bitcast.47), custom_call_target="tpu_custom_call" | custom-call | tf_op jit(solution)/shard_map/pallas_call | solution.py:369
  (130 shorter events, 26.5 us)
Async XLA Ops:
  7.2 249.8 %reduce-scatter.2.cloned.1.call-start = ((), (), s32[]{:S(2)}) async-start(), calls=%async_computation.1 | async-start | bytes 737280 | tf_op jit(solution)/shard_map/reduce_scatter | solution.py:542
  7.2 27.3 %collective-permute-start = (bf16[256,2048]{1,0:T(8,128)(2,1)}, bf16[256,2048]{1,0:T(8,128)(2,1)S(1)}, u32[]{:S(2)}, u32[]{:S(2)}) collective-permute-start(bf16[256,2048]{1,0:T(8,128)(2,1)} %param.15), channel_id=1, source_target_pairs={{0,2},{1,5},{2,0},{3,7},{4,6},{5,1},{6,4},{7,3},{8,10},{9,13},{10,... | collective-permute-start | bytes 3145736 | tf_op jit(solution)/shard_map/ppermute | solution.py:33
  10.2 24.3 %collective-permute-start.1 = (bf16[256,2048]{1,0:T(8,128)(2,1)}, bf16[256,2048]{1,0:T(8,128)(2,1)S(1)}, u32[]{:S(2)}, u32[]{:S(2)}) collective-permute-start(bf16[256,2048]{1,0:T(8,128)(2,1)} %param.21), channel_id=1, source_target_pairs={{0,2},{1,5},{2,0},{3,7},{4,6},{5,1},{6,4},{7,3},{8,10},{9,13},{10,... | collective-permute-start | bytes 3145736 | tf_op jit(solution)/shard_map/ppermute | solution.py:33
  12.9 5.4 %copy-start.10 = (s32[256,4]{0,1:T(4,128)S(1)}, s32[256,4]{0,1:T(4,128)}, u32[]{:S(2)}) copy-start(s32[256,4]{0,1:T(4,128)} %param.16) | copy-start | bytes 12292
  12.9 5.4 %copy-start.11 = (f32[256,4]{0,1:T(4,128)S(1)}, f32[256,4]{0,1:T(4,128)}, u32[]{:S(2)}) copy-start(f32[256,4]{0,1:T(4,128)} %param.17) | copy-start | bytes 12292
  18.3 26.7 %copy-start.6 = (bf16[256,2048]{1,0:T(8,128)(2,1)S(1)}, bf16[256,2048]{1,0:T(8,128)(2,1)}, u32[]{:S(2)}) copy-start(bf16[256,2048]{1,0:T(8,128)(2,1)} %param.15) | copy-start | bytes 3145732
  18.3 2.3 collective-permute-start.3
  18.3 16.2 %collective-permute-start.2 = (f32[8,256]{1,0:T(8,128)S(1)}, f32[8,256]{1,0:T(8,128)S(1)}, u32[]{:S(2)}, u32[]{:S(2)}) collective-permute-start(f32[8,256]{1,0:T(8,128)S(1)} %bitcast.66), channel_id=1, source_target_pairs={{0,2},{1,5},{2,0},{3,7},{4,6},{5,1},{6,4},{7,3},{8,10},{9,13},{10,... | collective-permute-start | bytes 24584 | tf_op jit(solution)/shard_map/ppermute | solution.py:33
  34.5 8.6 %copy-start.7 = (bf16[256,2048]{1,0:T(8,128)(2,1)}, bf16[256,2048]{1,0:T(8,128)(2,1)S(1)}, u32[]{:S(2)}) copy-start(bf16[256,2048]{1,0:T(8,128)(2,1)S(1)} %collective-permute-done) | copy-start | bytes 3145732
  34.5 8.6 %copy-start.8 = (bf16[256,2048]{1,0:T(8,128)(2,1)}, bf16[256,2048]{1,0:T(8,128)(2,1)S(1)}, u32[]{:S(2)}) copy-start(bf16[256,2048]{1,0:T(8,128)(2,1)S(1)} %collective-permute-done.1) | copy-start | bytes 3145732
  34.6 8.4 %collective-permute-start.5 = (bf16[3,2,48,512]{3,2,1,0:T(8,128)(2,1)S(1)}, bf16[3,2,48,512]{3,2,1,0:T(8,128)(2,1)S(1)}, u32[]{:S(2)}, u32[]{:S(2)}) collective-permute-start(bf16[3,2,48,512]{3,2,1,0:T(8,128)(2,1)S(1)} %dynamic-slice_bitcast_fusion.1), channel_id=1, source_target_pairs={{0,2},{1,3},{2,0},{3,1},{4,6},{5,7},{6,4},{7,5},{8,10},{9,11},{10,... | collective-permute-start | bytes 884744 | tf_op jit(solution)/shard_map/ppermute | solution.py:33
  37.3 11.2 %collective-permute-start.4 = (f32[8,512]{1,0:T(8,128)S(1)}, f32[8,512]{1,0:T(8,128)S(1)}, u32[]{:S(2)}, u32[]{:S(2)}) collective-permute-start(f32[8,512]{1,0:T(8,128)S(1)} %pad_maximum_fusion.4), channel_id=1, source_target_pairs={{0,4},{1,3},{2,6},{3,1},{4,0},{5,7},{6,2},{7,5},{8,12},{9,11},{10,... | collective-permute-start | bytes 49160 | tf_op jit(solution)/shard_map/ppermute | solution.py:33
  43.1 5.4 %collective-permute-start.6 = (bf16[3,1,48,512]{3,2,1,0:T(8,128)(2,1)S(1)}, bf16[3,1,48,512]{3,2,1,0:T(8,128)(2,1)S(1)}, u32[]{:S(2)}, u32[]{:S(2)}) collective-permute-start(bf16[3,1,48,512]{3,2,1,0:T(8,128)(2,1)S(1)} %constant_dynamic-slice_fusion.15), channel_id=1, source_target_pairs={{0,4},{1,5},{2,6},{3,7},{4,0},{5,1},{6,2},{7,3},{8,12},{9,13},{10,... | collective-permute-start | bytes 442376 | tf_op jit(solution)/shard_map/ppermute | solution.py:33
  48.5 26.5 %copy-start = (bf16[512,2048]{1,0:T(8,128)(2,1)}, bf16[512,2048]{1,0:T(8,128)(2,1)S(1)}, u32[]{:S(2)}) copy-start(bf16[512,2048]{1,0:T(8,128)(2,1)S(1)} %get-tuple-element.135.a_ref.xa_ref) | copy-start | bytes 6291460
  48.6 4.1 %collective-permute-start.10 = (f32[8,1024]{1,0:T(8,128)S(1)}, f32[8,1024]{1,0:T(8,128)S(1)}, u32[]{:S(2)}, u32[]{:S(2)}) collective-permute-start(f32[8,1024]{1,0:T(8,128)S(1)} %constant_dynamic-update-slice_fusion), channel_id=1, source_target_pairs={{0,1},{1,0},{2,3},{3,2},{4,5},{5,4},{6,7},{7,6},{8,9},{9,8},{10,11... | collective-permute-start | bytes 98312 | tf_op jit(solution)/shard_map/ppermute | solution.py:33
  49.3 34.0 %collective-permute-start.9 = (bf16[512,2048]{1,0:T(8,128)(2,1)S(1)}, bf16[512,2048]{1,0:T(8,128)(2,1)}, u32[]{:S(2)}, u32[]{:S(2)}) collective-permute-start(bf16[512,2048]{1,0:T(8,128)(2,1)S(1)} %get-tuple-element.135.a_ref.xa_ref), channel_id=1, source_target_pairs={{0,1},{1,0},{2,3},{3,2},{4,5},{5,4},{6,7},{7,6},{8,9},{9,8},{10,11... | collective-permute-start | bytes 6291464 | tf_op jit(solution)/shard_map/ppermute | solution.py:33
  49.9 62.4 %collective-permute-start.7 = (bf16[512,2048]{1,0:T(8,128)(2,1)S(1)}, bf16[512,2048]{1,0:T(8,128)(2,1)}, u32[]{:S(2)}, u32[]{:S(2)}) collective-permute-start(bf16[512,2048]{1,0:T(8,128)(2,1)S(1)} %get-tuple-element.135.a_ref.xa_ref), channel_id=1, source_target_pairs={{0,4},{1,3},{2,6},{3,1},{4,0},{5,7},{6,2},{7,5},{8,12},{9,11},{10,... | collective-permute-start | bytes 6291464 | tf_op jit(solution)/shard_map/ppermute | solution.py:33
  51.4 46.0 %collective-permute-start.13 = (bf16[512,2048]{1,0:T(8,128)(2,1)}, bf16[512,2048]{1,0:T(8,128)(2,1)}, u32[]{:S(2)}, u32[]{:S(2)}) collective-permute-start(bf16[512,2048]{1,0:T(8,128)(2,1)} %get-tuple-element.138.a_ref.ca_ref), channel_id=1, source_target_pairs={{0,1},{1,0},{2,3},{3,2},{4,5},{5,4},{6,7},{7,6},{8,9},{9,8},{10,11... | collective-permute-start | bytes 6291464 | tf_op jit(solution)/shard_map/ppermute | solution.py:33
  51.4 60.9 %collective-permute-start.8 = (bf16[512,2048]{1,0:T(8,128)(2,1)}, bf16[512,2048]{1,0:T(8,128)(2,1)}, u32[]{:S(2)}, u32[]{:S(2)}) collective-permute-start(bf16[512,2048]{1,0:T(8,128)(2,1)} %get-tuple-element.138.a_ref.ca_ref), channel_id=1, source_target_pairs={{0,4},{1,3},{2,6},{3,1},{4,0},{5,7},{6,2},{7,5},{8,12},{9,11},{10,... | collective-permute-start | bytes 6291464 | tf_op jit(solution)/shard_map/ppermute | solution.py:33
  52.7 6.2 %collective-permute-start.11 = (bf16[1,144,512]{2,1,0:T(8,128)(2,1)S(1)}, bf16[1,144,512]{2,1,0:T(8,128)(2,1)S(1)}, u32[]{:S(2)}, u32[]{:S(2)}) collective-permute-start(bf16[1,144,512]{2,1,0:T(8,128)(2,1)S(1)} %bitcast.57), channel_id=1, source_target_pairs={{0,8},{8,0},{16,24},{24,16},{1,9},{9,1},{17,25},{25,17},{2,10},{10... | collective-permute-start | bytes 442376 | tf_op jit(solution)/shard_map/ppermute | solution.py:78
  59.0 16.0 %collective-permute-start.12 = (bf16[2,144,512]{2,1,0:T(8,128)(2,1)S(1)}, bf16[2,144,512]{2,1,0:T(8,128)(2,1)S(1)}, u32[]{:S(2)}, u32[]{:S(2)}) collective-permute-start(bf16[2,144,512]{2,1,0:T(8,128)(2,1)S(1)} %pad_maximum_fusion.3), channel_id=1, source_target_pairs={{0,16},{8,24},{16,0},{24,8},{1,17},{9,25},{17,1},{25,9},{2,18},{10... | collective-permute-start | bytes 884744 | tf_op jit(solution)/shard_map/ppermute | solution.py:78
  112.3 12.0 %collective-permute-start.14 = (bf16[512,2048]{1,0:T(8,128)(2,1)}, bf16[512,2048]{1,0:T(8,128)(2,1)S(1)}, u32[]{:S(2)}, u32[]{:S(2)}) collective-permute-start(bf16[512,2048]{1,0:T(8,128)(2,1)} %collective-permute-done.7.a_ref.xa_ref), channel_id=1, source_target_pairs={{0,1},{1,0},{2,3},{3,2},{4,5},{5,4},{6,7},{7,6},{8,9},{9,8},{10,11... | collective-permute-start | bytes 6291464 | tf_op jit(solution)/shard_map/ppermute | solution.py:33
  112.4 12.0 %collective-permute-start.15 = (bf16[512,2048]{1,0:T(8,128)(2,1)}, bf16[512,2048]{1,0:T(8,128)(2,1)}, u32[]{:S(2)}, u32[]{:S(2)}) collective-permute-start(bf16[512,2048]{1,0:T(8,128)(2,1)} %collective-permute-done.8.a_ref.ca_ref), channel_id=1, source_target_pairs={{0,1},{1,0},{2,3},{3,2},{4,5},{5,4},{6,7},{7,6},{8,9},{9,8},{10,11... | collective-permute-start | bytes 6291464 | tf_op jit(solution)/shard_map/ppermute | solution.py:33
  124.4 1.4 copy-start.1
  124.4 48.8 %collective-permute-start.18 = (bf16[512,2048]{1,0:T(8,128)(2,1)}, bf16[512,2048]{1,0:T(8,128)(2,1)}, u32[]{:S(2)}, u32[]{:S(2)}) collective-permute-start(bf16[512,2048]{1,0:T(8,128)(2,1)} %get-tuple-element.162), channel_id=1, source_target_pairs={{0,1},{1,0},{2,3},{3,2},{4,5},{5,4},{6,7},{7,6},{8,9},{9,8},{10,11... | collective-permute-start | bytes 6291464 | tf_op jit(solution)/shard_map/ppermute | solution.py:33
  124.5 48.7 %collective-permute-start.19 = (bf16[512,2048]{1,0:T(8,128)(2,1)}, bf16[512,2048]{1,0:T(8,128)(2,1)}, u32[]{:S(2)}, u32[]{:S(2)}) collective-permute-start(bf16[512,2048]{1,0:T(8,128)(2,1)} %get-tuple-element.164), channel_id=1, source_target_pairs={{0,1},{1,0},{2,3},{3,2},{4,5},{5,4},{6,7},{7,6},{8,9},{9,8},{10,11... | collective-permute-start | bytes 6291464 | tf_op jit(solution)/shard_map/ppermute | solution.py:33
  154.7 18.5 %collective-permute-start.17 = (bf16[512,2048]{1,0:T(8,128)(2,1)}, bf16[512,2048]{1,0:T(8,128)(2,1)S(1)}, u32[]{:S(2)}, u32[]{:S(2)}) collective-permute-start(bf16[512,2048]{1,0:T(8,128)(2,1)} %get-tuple-element.158), channel_id=1, source_target_pairs={{0,1},{1,0},{2,3},{3,2},{4,5},{5,4},{6,7},{7,6},{8,9},{9,8},{10,11... | collective-permute-start | bytes 6291464 | tf_op jit(solution)/shard_map/ppermute | solution.py:33
  154.8 18.4 %collective-permute-start.16 = (bf16[512,2048]{1,0:T(8,128)(2,1)}, bf16[512,2048]{1,0:T(8,128)(2,1)}, u32[]{:S(2)}, u32[]{:S(2)}) collective-permute-start(bf16[512,2048]{1,0:T(8,128)(2,1)} %get-tuple-element.156), channel_id=1, source_target_pairs={{0,1},{1,0},{2,3},{3,2},{4,5},{5,4},{6,7},{7,6},{8,9},{9,8},{10,11... | collective-permute-start | bytes 6291464 | tf_op jit(solution)/shard_map/ppermute | solution.py:33
  173.2 9.7 %copy-start.3 = (bf16[512,2048]{1,0:T(8,128)(2,1)}, bf16[512,2048]{1,0:T(8,128)(2,1)S(1)}, u32[]{:S(2)}) copy-start(bf16[512,2048]{1,0:T(8,128)(2,1)S(1)} %collective-permute-done.17.refs_1_) | copy-start | bytes 6291460
  173.2 36.0 %collective-permute-start.20 = (bf16[1152,512]{1,0:T(8,128)(2,1)}, bf16[1152,512]{1,0:T(8,128)(2,1)}, u32[]{:S(2)}, u32[]{:S(2)}) collective-permute-start(bf16[1152,512]{1,0:T(8,128)(2,1)} %get-tuple-element.171), channel_id=1, source_target_pairs={{0,8},{1,9},{2,10},{3,11},{4,12},{5,13},{6,14},{7,15}} | collective-permute-start | bytes 3538952 | tf_op jit(solution)/shard_map/ppermute | solution.py:69
  176.7 32.5 %collective-permute-start.21 = (bf16[1152,512]{1,0:T(8,128)(2,1)S(1)}, bf16[1152,512]{1,0:T(8,128)(2,1)}, u32[]{:S(2)}, u32[]{:S(2)}) collective-permute-start(bf16[1152,512]{1,0:T(8,128)(2,1)S(1)} %get-tuple-element.172), channel_id=1, source_target_pairs={{24,16},{25,17},{26,18},{27,19},{28,20},{29,21},{30,22},{31,23}} | collective-permute-start | bytes 3538952 | tf_op jit(solution)/shard_map/ppermute | solution.py:70
  182.9 15.1 %collective-permute-start.22 = (bf16[256,2048]{1,0:T(8,128)(2,1)}, bf16[256,2048]{1,0:T(8,128)(2,1)}, u32[]{:S(2)}, u32[]{:S(2)}) collective-permute-start(bf16[256,2048]{1,0:T(8,128)(2,1)} %get-tuple-element.175), channel_id=1, source_target_pairs={{0,4},{1,3},{2,6},{3,1},{4,0},{5,7},{6,2},{7,5},{8,12},{9,11},{10,... | collective-permute-start | bytes 3145736 | tf_op jit(solution)/shard_map/ppermute | solution.py:33
  183.1 26.1 %collective-permute-start.23 = (bf16[256,2048]{1,0:T(8,128)(2,1)}, bf16[256,2048]{1,0:T(8,128)(2,1)}, u32[]{:S(2)}, u32[]{:S(2)}) collective-permute-start(bf16[256,2048]{1,0:T(8,128)(2,1)} %get-tuple-element.176), channel_id=1, source_target_pairs={{0,4},{1,3},{2,6},{3,1},{4,0},{5,7},{6,2},{7,5},{8,12},{9,11},{10,... | collective-permute-start | bytes 3145736 | tf_op jit(solution)/shard_map/ppermute | solution.py:33
  197.9 15.4 %copy-start.2 = (bf16[512,2048]{1,0:T(8,128)(2,1)S(1)}, bf16[512,2048]{1,0:T(8,128)(2,1)}, u32[]{:S(2)}) copy-start(bf16[512,2048]{1,0:T(8,128)(2,1)} %shard_map.198) | copy-start | bytes 6291460
  213.3 43.7 %collective-permute-start.25 = (bf16[512,2048]{1,0:T(8,128)(2,1)S(1)}, bf16[512,2048]{1,0:T(8,128)(2,1)}, u32[]{:S(2)}, u32[]{:S(2)}) collective-permute-start(bf16[512,2048]{1,0:T(8,128)(2,1)S(1)} %copy-done.2), channel_id=1, source_target_pairs={{0,4},{1,3},{2,6},{3,1},{4,0},{5,7},{6,2},{7,5},{8,12},{9,11},{10,... | collective-permute-start | bytes 6291464 | tf_op jit(solution)/shard_map/ppermute | solution.py:33
  215.4 8.8 %copy-start.13 = (s32[8]{0:T(128)S(1)}, s32[8]{0:T(128)}, u32[]{:S(2)}) copy-start(s32[8]{0:T(128)} %constant.132.clone) | copy-start | bytes 100
  215.4 12.0 %copy-start.12 = (s32[8]{0:T(128)S(1)}, s32[8]{0:T(128)}, u32[]{:S(2)}) copy-start(s32[8]{0:T(128)} %constant.131.clone) | copy-start | bytes 100
  215.4 70.9 %all-gather.5.cloned.1.call-start = ((), (), s32[]{:S(2)}) async-start(), calls=%async_computation.2 | async-start | bytes 1327104 | tf_op jit(solution)/shard_map/all_gather | solution.py:562
  215.5 41.4 %collective-permute-start.26 = (bf16[1152,512]{1,0:T(8,128)(2,1)}, bf16[1152,512]{1,0:T(8,128)(2,1)}, u32[]{:S(2)}, u32[]{:S(2)}) collective-permute-start(bf16[1152,512]{1,0:T(8,128)(2,1)} %get-tuple-element.192), channel_id=1, source_target_pairs={{0,8},{8,16},{1,9},{9,17},{2,10},{10,18},{3,11},{11,19},{4,12},{12... | collective-permute-start | bytes 3538952 | tf_op jit(solution)/shard_map/ppermute | solution.py:69
  217.8 39.1 %collective-permute-start.27 = (bf16[1152,512]{1,0:T(8,128)(2,1)S(1)}, bf16[1152,512]{1,0:T(8,128)(2,1)}, u32[]{:S(2)}, u32[]{:S(2)}) collective-permute-start(bf16[1152,512]{1,0:T(8,128)(2,1)S(1)} %get-tuple-element.193), channel_id=1, source_target_pairs={{24,16},{16,8},{25,17},{17,9},{26,18},{18,10},{27,19},{19,11},{28,... | collective-permute-start | bytes 3538952 | tf_op jit(solution)/shard_map/ppermute | solution.py:70
  224.1 30.4 %collective-permute-start.24 = (bf16[256,2048]{1,0:T(8,128)(2,1)}, bf16[256,2048]{1,0:T(8,128)(2,1)}, u32[]{:S(2)}, u32[]{:S(2)}) collective-permute-start(bf16[256,2048]{1,0:T(8,128)(2,1)} %get-tuple-element.187), channel_id=1, source_target_pairs={{0,2},{1,5},{2,0},{3,7},{4,6},{5,1},{6,4},{7,3},{8,10},{9,13},{10,... | collective-permute-start | bytes 3145736 | tf_op jit(solution)/shard_map/ppermute | solution.py:33
  261.0 9.1 %copy-start.9 = (f32[8,2,2048]{2,1,0:T(2,128)S(1)}, f32[8,2,2048]{2,1,0:T(2,128)}, u32[]{:S(2)}) copy-start(f32[8,2,2048]{2,1,0:T(2,128)} %all-gather.2) | copy-start | bytes 393220
  265.6 18.3 %collective-permute-start.28 = (bf16[256,2048]{1,0:T(8,128)(2,1)}, bf16[256,2048]{1,0:T(8,128)(2,1)}, u32[]{:S(2)}, u32[]{:S(2)}) collective-permute-start(bf16[256,2048]{1,0:T(8,128)(2,1)} %get-tuple-element.202), channel_id=1, source_target_pairs={{0,2},{1,5},{2,0},{3,7},{4,6},{5,1},{6,4},{7,3},{8,10},{9,13},{10,... | collective-permute-start | bytes 3145736 | tf_op jit(solution)/shard_map/ppermute | solution.py:33
  267.5 27.6 %collective-permute-start.29 = (bf16[1152,512]{1,0:T(8,128)(2,1)}, bf16[1152,512]{1,0:T(8,128)(2,1)S(1)}, u32[]{:S(2)}, u32[]{:S(2)}) collective-permute-start(bf16[1152,512]{1,0:T(8,128)(2,1)} %get-tuple-element.204), channel_id=1, source_target_pairs={{0,8},{8,16},{16,24},{1,9},{9,17},{17,25},{2,10},{10,18},{18,26},{... | collective-permute-start | bytes 3538952 | tf_op jit(solution)/shard_map/ppermute | solution.py:69
  268.9 30.1 %collective-permute-start.30 = (bf16[1152,512]{1,0:T(8,128)(2,1)S(1)}, bf16[1152,512]{1,0:T(8,128)(2,1)S(1)}, u32[]{:S(2)}, u32[]{:S(2)}) collective-permute-start(bf16[1152,512]{1,0:T(8,128)(2,1)S(1)} %get-tuple-element.205), channel_id=1, source_target_pairs={{24,16},{16,8},{8,0},{25,17},{17,9},{9,1},{26,18},{18,10},{10,2},{... | collective-permute-start | bytes 3538952 | tf_op jit(solution)/shard_map/ppermute | solution.py:70
  295.1 3.9 %copy-start.4 = (bf16[1152,512]{1,0:T(8,128)(2,1)}, bf16[1152,512]{1,0:T(8,128)(2,1)S(1)}, u32[]{:S(2)}) copy-start(bf16[1152,512]{1,0:T(8,128)(2,1)S(1)} %collective-permute-done.29.right_ref) | copy-start | bytes 3538948
  298.9 1.0 copy-start.5
Sparse Core Ops, SparseCore 0:
  215.5 28.2 reduce-scatter.1
  257.1 25.6 all-gather.4
